TPU v7x, 32 devices: a whole 2x2x4 slice. The times are simulated.
32 devices in a mesh: ep: 8 (over y, x, core), ex: 4 (over z).
Axes of the slice: x: 2, y: 2, z: 4, core: 2. Of those that a mesh axis runs over, the one named last changes fastest.
Arguments:
- dout: bfloat16 [1024, 7168], P(('ep', 'ex')), may hold values from -1.5 to 1.5
- gates: bfloat16 [1024, 8], P(('ep', 'ex')), may hold values from 0.049804688 to 0.59765625
- saved_down_input: bfloat16 [1024, 8, 1024], P(('ep', 'ex')), may hold values from -3 to 3
- routing: int32 [1024, 8], P(('ep', 'ex')), may hold values from 0 to 27, as said below
- placement: int32 [32], replicated, may hold values from 0 to 27, as said below
- partner: int32 [32], replicated, may hold values from 0 to 31, as said below
- frozen: bfloat16 [32, 1024, 7168], P(('ep', 'ex')), as said below
- colscale: float32 [32, 7168], P(('ep', 'ex')), may hold values from 0.5 to 2, as said below
- adapter_down_factor: bfloat16 [32, 1024, 64], P(('ep', 'ex')), as said below
- adapter_up_factor: bfloat16 [32, 64, 7168], P(('ep', 'ex')), as said below
- first_moment_down: bfloat16 [32, 1024, 64], P(('ep', 'ex')), as said below
- second_moment_down: bfloat16 [32, 1024, 64], P(('ep', 'ex')), may hold values from 0.1 to 4, as said below
- first_moment_up: bfloat16 [32, 64, 7168], P(('ep', 'ex')), as said below
- second_moment_up: bfloat16 [32, 64, 7168], P(('ep', 'ex')), may hold values from 0.1 to 4, as said below
Outputs:
- routed_input_gradient: bfloat16 [1024, 8, 1024], P(('ep', 'ex'))
- combine_gate_gradient: bfloat16 [1024, 8], P(('ep', 'ex'))
- updated_down_factor: bfloat16 [32, 1024, 64], P(('ep', 'ex'))
- updated_up_factor: bfloat16 [32, 64, 7168], P(('ep', 'ex'))
- updated_first_moment_down: bfloat16 [32, 1024, 64], P(('ep', 'ex'))
- updated_second_moment_down: bfloat16 [32, 1024, 64], P(('ep', 'ex'))
- updated_first_moment_up: bfloat16 [32, 64, 7168], P(('ep', 'ex'))
- updated_second_moment_up: bfloat16 [32, 64, 7168], P(('ep', 'ex'))
Inputs may be any that keep to these rules, and one draw needn't show every extreme that they name: `routing`: each token names 8 different experts. Of each device's tokens, an expert with two slots is named by exactly 16, every other expert by exactly 8. `placement`: every expert is held by one slot, or by two slots of one expert group (equal index along ep); 4 experts hold two slots, each in a group of its own. placement[partner[s]] = placement[s]; partner[s] is the other slot of the same expert, or s if the expert holds one slot. `frozen`: slots of the same expert hold equal values. `colscale`: slots of the same expert hold equal values. `adapter_down_factor`: slots of the same expert hold equal values. `adapter_up_factor`: slots of the same expert hold equal values. `first_moment_down`: slots of the same expert hold equal values. `second_moment_down`: slots of the same expert hold equal values. `first_moment_up`: slots of the same expert hold equal values. `second_moment_up`: slots of the same expert hold equal values.
All inputs are finite; a program needn't handle non-finite values.
Results may differ from a plain program's by a relative error of at most 0.005.
Values may be sent and summed in bfloat16 or wider, within the bound.
No kernel may reach another device: no remote copies, remote signals or barrier semaphores. Data moves between devices by JAX's collectives and lax.ppermute only.
A program may use at most 128 MiB of HBM per device.

v0:
```python
import jax
import jax.numpy as jnp
from jax import lax
from jax.sharding import PartitionSpec as P

adapter_scale = 2.0
beta_one = 0.9
beta_two = 0.999
adam_eps = 1e-08
learn_rate = 0.01
weight_decay = 0.01
adam_step = 10


def expert_row_block(
    hidden_row_block,
    output_gradient_rows,
    gate_row_values,
    frozen_w,
    scale,
    adapter_down_projected,
    low_b,
):
    gate_broadcast_wide = gate_row_values.astype(jnp.float32)[:, None]
    dout_wide = output_gradient_rows.astype(jnp.float32)
    adapter_output_gradient = (gate_broadcast_wide * dout_wide).astype(jnp.bfloat16)
    dsc_low = (dout_wide * scale[None, :]).astype(jnp.bfloat16)
    backward_through_adapter = jnp.dot(
        adapter_output_gradient, low_b.T, preferred_element_type=jnp.float32
    ).astype(jnp.bfloat16)
    backward_through_frozen = jnp.dot(dsc_low, frozen_w.T, preferred_element_type=jnp.float32)
    incoming_input_gradient = (
        gate_broadcast_wide * backward_through_frozen
        + adapter_scale
        * jnp.dot(
            backward_through_adapter, adapter_down_projected.T, preferred_element_type=jnp.float32
        )
    )
    adapter_down_product = jnp.dot(
        hidden_row_block, adapter_down_projected, preferred_element_type=jnp.float32
    ).astype(jnp.bfloat16)
    output_gradient_adapter = jnp.dot(
        output_gradient_rows, low_b.T, preferred_element_type=jnp.float32
    )
    gated_output = jnp.sum(
        hidden_row_block.astype(jnp.float32) * backward_through_frozen, axis=1
    ) + adapter_scale * jnp.sum(
        adapter_down_product.astype(jnp.float32) * output_gradient_adapter, axis=1
    )
    down_factor_gradient = adapter_scale * jnp.dot(
        hidden_row_block.T, backward_through_adapter, preferred_element_type=jnp.float32
    )
    up_factor_gradient = adapter_scale * jnp.dot(
        adapter_down_product.T, adapter_output_gradient, preferred_element_type=jnp.float32
    )
    return (
        incoming_input_gradient.astype(jnp.bfloat16),
        gated_output.astype(jnp.bfloat16),
        down_factor_gradient,
        up_factor_gradient,
    )


def apply_adam_update(weights, moment, second_moment, gradient):
    weights_wide = weights.astype(jnp.float32)
    first = beta_one * moment.astype(jnp.float32) + (1.0 - beta_one) * gradient
    second = beta_two * second_moment.astype(jnp.float32) + (1.0 - beta_two) * gradient * gradient
    first_hat = first / (1.0 - beta_one**adam_step)
    second_hat = second / (1.0 - beta_two**adam_step)
    fresh = weights_wide - learn_rate * (
        first_hat / (jnp.sqrt(second_hat) + adam_eps) + weight_decay * weights_wide
    )
    return (fresh.astype(jnp.bfloat16), first.astype(jnp.bfloat16), second.astype(jnp.bfloat16))


def per_device(
    dout,
    gates,
    saved_down_input,
    routing,
    placement,
    partner,
    frozen,
    colscale,
    adapter_down_factor,
    adapter_up_factor,
    first_moment_down,
    second_moment_down,
    first_moment_up,
    second_moment_up,
):
    groups = lax.axis_size("ep")
    members = lax.axis_size("ex")
    slot_count = groups * members
    tok_rows, top_count = routing.shape
    model_width = dout.shape[1]
    hidden = saved_down_input.shape[2]
    adapter_rank_width = adapter_down_factor.shape[2]
    row_count = tok_rows * top_count
    capacity = row_count // slot_count
    expert_flat = routing.reshape(row_count)
    slot_ids = jnp.arange(slot_count, dtype=jnp.int32)
    holds_expert = placement[None, :] == expert_flat[:, None]
    first_slot = jnp.min(jnp.where(holds_expert, slot_ids[None, :], slot_count), axis=1)
    last_slot = jnp.max(jnp.where(holds_expert, slot_ids[None, :], -1), axis=1)
    row_ids = jnp.arange(row_count, dtype=jnp.int32)
    earlier = row_ids[None, :] < row_ids[:, None]
    same_expert = expert_flat[None, :] == expert_flat[:, None]
    turn_index = jnp.sum((same_expert & earlier).astype(jnp.int32), axis=1)
    target = jnp.where(turn_index % 2 == 1, last_slot, first_slot)
    same_slot = target[None, :] == target[:, None]
    position = jnp.sum((same_slot & earlier).astype(jnp.int32), axis=1)
    buffer_row = target * capacity + position
    row_width = model_width + hidden
    row_data = jnp.concatenate(
        [jnp.broadcast_to(dout[:, None, :], (tok_rows, top_count, model_width)), saved_down_input],
        axis=2,
    ).reshape(row_count, row_width)
    outgoing = (
        jnp.zeros((slot_count * capacity, row_width), jnp.bfloat16).at[buffer_row].set(row_data)
    )
    outgoing_gate = (
        jnp.zeros((slot_count * capacity,), jnp.bfloat16)
        .at[buffer_row]
        .set(gates.reshape(row_count))
    )
    incoming, incoming_gate = (
        lax.all_to_all(
            outgoing.reshape(slot_count, capacity, row_width),
            ("ep", "ex"),
            split_axis=0,
            concat_axis=0,
            tiled=True,
        ),
        lax.all_to_all(
            outgoing_gate.reshape(slot_count, capacity),
            ("ep", "ex"),
            split_axis=0,
            concat_axis=0,
            tiled=True,
        ),
    )
    live_rows = slot_count * capacity
    incoming = incoming.reshape(live_rows, row_width)
    output_gradient_rows = incoming[:, :model_width]
    hidden_row_block = incoming[:, model_width:]
    incoming_input_gradient, gated_output, down_factor_gradient, up_factor_gradient = (
        expert_row_block(
            hidden_row_block,
            output_gradient_rows,
            incoming_gate.reshape(live_rows),
            frozen[0],
            colscale[0],
            adapter_down_factor[0],
            adapter_up_factor[0],
        )
    )
    returned_grad, returned_gate = (
        lax.all_to_all(
            incoming_input_gradient.reshape(slot_count, capacity, hidden),
            ("ep", "ex"),
            split_axis=0,
            concat_axis=0,
            tiled=True,
        ),
        lax.all_to_all(
            gated_output.reshape(slot_count, capacity),
            ("ep", "ex"),
            split_axis=0,
            concat_axis=0,
            tiled=True,
        ),
    )
    routed_input_gradient = returned_grad.reshape(live_rows, hidden)[buffer_row].reshape(
        tok_rows, top_count, hidden
    )
    combine_gate_gradient = returned_gate.reshape(live_rows)[buffer_row].reshape(
        tok_rows, top_count
    )
    own_member = lax.axis_index("ex")
    own_slot = lax.axis_index("ep") * members + own_member
    mate_slot = jnp.sum(jnp.where(slot_ids == own_slot, partner, 0))
    mate_member = mate_slot % members
    flat_a = down_factor_gradient.reshape(1, hidden * adapter_rank_width // 128, 128)
    flat_b = up_factor_gradient.reshape(1, adapter_rank_width, model_width)
    pieces = (
        lax.all_gather(flat_a.astype(jnp.bfloat16), "ex", axis=0, tiled=True).astype(jnp.float32),
        lax.all_gather(flat_b.astype(jnp.bfloat16), "ex", axis=0, tiled=True).astype(jnp.float32),
    )
    length = pieces[0].shape[0]
    members_here = jnp.arange(length, dtype=jnp.int32)
    chosen = ((members_here == own_member) | (members_here == mate_member)).astype(jnp.float32)
    summed_down_gradient = jnp.zeros(flat_a.shape[1:], jnp.float32) + jnp.sum(
        chosen[:, None, None] * pieces[0], axis=0
    )
    summed_up_gradient = jnp.zeros(flat_b.shape[1:], jnp.float32) + jnp.sum(
        chosen[:, None, None] * pieces[1], axis=0
    )
    summed_down_gradient = summed_down_gradient.reshape(1, hidden, adapter_rank_width)
    summed_up_gradient = summed_up_gradient.reshape(1, adapter_rank_width, model_width)
    updated_down_factor, updated_first_moment_down, updated_second_moment_down = apply_adam_update(
        adapter_down_factor, first_moment_down, second_moment_down, summed_down_gradient
    )
    updated_up_factor, updated_first_moment_up, updated_second_moment_up = apply_adam_update(
        adapter_up_factor, first_moment_up, second_moment_up, summed_up_gradient
    )
    return (
        routed_input_gradient,
        combine_gate_gradient,
        updated_down_factor,
        updated_up_factor,
        updated_first_moment_down,
        updated_second_moment_down,
        updated_first_moment_up,
        updated_second_moment_up,
    )


def solution(mesh):
    placed = (
        P(("ep", "ex"), None),
        P(("ep", "ex"), None),
        P(("ep", "ex"), None, None),
        P(("ep", "ex"), None),
        P(),
        P(),
        P(("ep", "ex"), None, None),
        P(("ep", "ex"), None),
        P(("ep", "ex"), None, None),
        P(("ep", "ex"), None, None),
        P(("ep", "ex"), None, None),
        P(("ep", "ex"), None, None),
        P(("ep", "ex"), None, None),
        P(("ep", "ex"), None, None),
    )
    return jax.shard_map(
        per_device,
        mesh=mesh,
        in_specs=placed,
        out_specs=(
            P(("ep", "ex"), None, None),
            P(("ep", "ex"), None),
            P(("ep", "ex"), None, None),
            P(("ep", "ex"), None, None),
            P(("ep", "ex"), None, None),
            P(("ep", "ex"), None, None),
            P(("ep", "ex"), None, None),
            P(("ep", "ex"), None, None),
        ),
        check_vma=False,
    )
```

profile of v0, /device:TPU:0, one launch (start us, length us, event | category | flops | bytes accessed | tf_op | source)
XLA Modules:
  0.0 243.8 jit_solution(11940484604645975405)
XLA Ops:
  7.2 0.8 copy.56
  10.1 2.2 scatter_custom_fusion
  13.0 7.3 %all-to-all-start = ((bf16[32,1,8]{2,1,0:T(2,128)(2,1)}), bf16[32,1,8]{2,1,0:T(2,128)(2,1)S(1)}, u32[]{:S(2)}, u32[]{:S(2)}) async-start(bf16[32,1,8]{2,1,0:T(2,128)(2,1)} %all_to_all.21), calls=%async_computation | async-start | bytes 32768 | tf_op jit(solution)/shard_map/all_to_all | solution.py:135
  20.3 3.3 %broadcast_in_dim.56 = bf16[32,8,7168]{2,1,0:T(8,128)(2,1)} broadcast(bf16[32,7168]{1,0:T(8,128)(2,1)} %param.14), dimensions={0,2} | broadcast | bytes 4128768 | tf_op jit(solution)/shard_map/broadcast_in_dim | solution.py:116
  23.6 10.0 %scatter_custom_fusion.1 = bf16[256,8192]{1,0:T(8,128)(2,1)} fusion(s32[256]{0:T(256)S(1)} %bitcast.56, bf16[32,8,1024]{2,1,0:T(8,128)(2,1)S(1)} %copy-done.3, bf16[]{:T(256)} %constant.102, bf16[32,8,7168]{2,1,0:T(8,128)(2,1)} %broadcast_in_dim.56, bf16[]{:T(256)} %constant.25.clone.1), kind=kCustom, calls=%fused_computation.15 | custom fusion | flops 8388608 | bytes 8388612 | tf_op jit(solution)/shard_map/scatter | solution.py:120
  33.6 6.0 %all-to-all-start.1 = ((bf16[32,8,8192]{2,1,0:T(8,128)(2,1)}), bf16[32,8,8192]{2,1,0:T(8,128)(2,1)}, u32[]{:S(2)}, u32[]{:S(2)}) async-start(bf16[32,8,8192]{2,1,0:T(8,128)(2,1)} %bitcast.49), calls=%async_computation.1 | async-start | bytes 8388608 | tf_op jit(solution)/shard_map/all_to_all | solution.py:128
  39.9 91.9 %all-to-all-done.1 = bf16[32,8,8192]{2,1,0:T(8,128)(2,1)} async-done(((bf16[32,8,8192]{2,1,0:T(8,128)(2,1)}), bf16[32,8,8192]{2,1,0:T(8,128)(2,1)}, u32[]{:S(2)}, u32[]{:S(2)}) %all-to-all-start.1) | async-done | bytes 4194336 | tf_op jit(solution)/shard_map/all_to_all | solution.py:128
  131.8 1.3 convolution_convert_fusion
  133.2 4.1 %fusion.2 = bf16[64,7168]{1,0:T(8,128)(2,1)} fusion(bf16[256,64]{0,1:T(8,128)(2,1)S(1)} %convolution_convert_fusion, f32[256]{0:T(256)S(1)} %reshape.282, bf16[256,8192]{1,0:T(8,128)(2,1)} %bitcast.7), kind=kOutput, calls=%fused_computation.9 | convolution fusion | flops 241303552 | bytes 4621312 | tf_op jit(solution)/shard_map/dot_general | solution.py:53
  139.9 3.3 %fusion.27 = f32[256]{0:T(256)S(1)} fusion(bf16[256,8192]{1,0:T(8,128)(2,1)} %bitcast.7, bf16[1,64,7168]{2,1,0:T(8,128)(2,1)S(1)} %copy-done, bf16[256,64]{0,1:T(8,128)(2,1)S(1)} %convolution_convert_fusion), kind=kOutput, calls=%fused_computation.41 | convolution fusion | flops 234929920 | bytes 4621312 | tf_op jit(solution)/shard_map/dot_general | solution.py:42
  143.2 11.3 %multiply_reduce_fusion.1 = (f32[256]{0:T(256)S(1)}, f32[256,1024]{1,0:T(8,128)S(1)}) fusion(bf16[256,8192]{1,0:T(8,128)(2,1)} %bitcast.7, bf16[1,1024,7168]{2,1,0:T(8,128)(2,1)} %param.20, f32[7168]{0:T(1024)S(1)} %bitcast.59), kind=kOutput, calls=%fused_computation.44 | convolution fusion | flops 3764387584 | bytes 19952640 | tf_op jit(solution)/shard_map/dot_general | solution.py:31
  155.1 5.4 %all-to-all-start.3 = ((bf16[32,1,8]{2,1,0:T(2,128)(2,1)}), bf16[32,1,8]{2,1,0:T(2,128)(2,1)S(1)}, u32[]{:S(2)}, u32[]{:S(2)}) async-start(bf16[32,1,8]{2,1,0:T(2,128)(2,1)} %convert_element_type.158), calls=%async_computation.3 | async-start | bytes 32768 | tf_op jit(solution)/shard_map/all_to_all | solution.py:166
  160.5 3.3 %convolution_convert_fusion.1 = bf16[256,64]{0,1:T(8,128)(2,1)S(1)} fusion(f32[256]{0:T(256)S(1)} %reshape.282, bf16[256,8192]{1,0:T(8,128)(2,1)} %bitcast.7, bf16[1,64,7168]{2,1,0:T(8,128)(2,1)S(1)} %copy-done), kind=kOutput, calls=%fused_computation.40 | convolution fusion | flops 240402432 | bytes 4621312 | tf_op jit(solution)/shard_map/dot_general | solution.py:28
  163.9 1.1 fusion.22
  165.0 2.9 %all-to-all-done.3 = bf16[32,1,8]{2,1,0:T(2,128)(2,1)S(1)} async-done(((bf16[32,1,8]{2,1,0:T(2,128)(2,1)}), bf16[32,1,8]{2,1,0:T(2,128)(2,1)S(1)}, u32[]{:S(2)}, u32[]{:S(2)}) %all-to-all-start.3) | async-done | bytes 544 | tf_op jit(solution)/shard_map/all_to_all | solution.py:166
  167.9 3.0 %all-to-all-start.2 = ((bf16[32,8,1024]{2,1,0:T(8,128)(2,1)}), bf16[32,8,1024]{2,1,0:T(8,128)(2,1)S(1)}, u32[]{:S(2)}, u32[]{:S(2)}) async-start(bf16[32,8,1024]{2,1,0:T(8,128)(2,1)} %fusion.22), calls=%async_computation.2 | async-start | bytes 1048576 | tf_op jit(solution)/shard_map/all_to_all | solution.py:159
  170.9 1.3 fusion.23
  172.5 41.9 %all_gather.6 = bf16[4,512,128]{2,1,0:T(8,128)(2,1)S(1)} all-gather(bf16[1,512,128]{2,1,0:T(8,128)(2,1)S(1)} %convert_element_type.141), channel_id=1, replica_groups=mesh['ep'=8,'ex'=4] {'ex'}, dimensions={0}, use_global_device_ids=true | all-gather | bytes 655360 | tf_op jit(solution)/shard_map/all_gather | solution.py:187
  214.9 1.0 fusion.45
  216.1 1.9 gather_fusion.1
  218.8 2.0 gather_fusion
  220.7 9.4 %all-gather.3.cloned.1.call-done = bf16[256,7168]{1,0:T(8,128)(2,1)} async-done(((bf16[64,7168]{1,0:T(8,128)(2,1)}), bf16[256,7168]{1,0:T(8,128)(2,1)}) %all-gather.3.cloned.1.call-update) | async-done | bytes 3670032 | tf_op jit(solution)/shard_map/all_gather | solution.py:188
  230.2 3.1 %fusion.5 = f32[64,7168]{1,0:T(8,128)S(1)} fusion(bf16[4,64,7168]{2,1,0:T(8,128)(2,1)} %bitcast.50, f32[4]{0:T(128)S(1)} %or_convert_fusion), kind=kLoop, calls=%fused_computation.13 | loop fusion | flops 5046272 | bytes 5505040 | tf_op jit(solution)/shard_map/reduce_sum | solution.py:196
  233.3 3.7 %fusion.33 = (bf16[1,64,7168]{2,1,0:T(8,128)(2,1)}, bf16[1,64,7168]{2,1,0:T(8,128)(2,1)}, bf16[1,64,7168]{2,1,0:T(8,128)(2,1)}) fusion(f32[64,7168]{1,0:T(8,128)S(1)} %fusion.5, bf16[1,64,7168]{2,1,0:T(8,128)(2,1)S(1)} %copy-done.1, bf16[1,64,7168]{2,1,0:T(8,128)(2,1)S(1)} %copy-done.2, bf16[1,64,7168]{2,1,0:T(8,128)(2,1)S(1)} %copy-done), kind=kLoop, calls=%fused_computation.45 | loop fusion | flops 9633792 | bytes 7340032 | tf_op jit(solution)/shard_map/convert_element_type | solution.py:73
  (47 shorter events, 6.3 us)
Async XLA Ops:
  7.2 16.5 %copy-start.3 = (bf16[32,8,1024]{2,1,0:T(8,128)(2,1)S(1)}, bf16[32,8,1024]{2,1,0:T(8,128)(2,1)}, u32[]{:S(2)}) copy-start(bf16[32,8,1024]{2,1,0:T(8,128)(2,1)} %param.16) | copy-start | bytes 1572868
  13.0 20.6 %all-to-all-start = ((bf16[32,1,8]{2,1,0:T(2,128)(2,1)}), bf16[32,1,8]{2,1,0:T(2,128)(2,1)S(1)}, u32[]{:S(2)}, u32[]{:S(2)}) async-start(bf16[32,1,8]{2,1,0:T(2,128)(2,1)} %all_to_all.21), calls=%async_computation | async-start | bytes 32768 | tf_op jit(solution)/shard_map/all_to_all | solution.py:135
  33.6 98.2 %copy-start.4 = (bf16[1,1024,64]{1,2,0:T(8,128)(2,1)S(1)}, bf16[1,1024,64]{1,2,0:T(8,128)(2,1)}, u32[]{:S(2)}) copy-start(bf16[1,1024,64]{1,2,0:T(8,128)(2,1)} %param.22) | copy-start | bytes 393220
  33.6 98.2 %all-to-all-start.1 = ((bf16[32,8,8192]{2,1,0:T(8,128)(2,1)}), bf16[32,8,8192]{2,1,0:T(8,128)(2,1)}, u32[]{:S(2)}, u32[]{:S(2)}) async-start(bf16[32,8,8192]{2,1,0:T(8,128)(2,1)} %bitcast.49), calls=%async_computation.1 | async-start | bytes 8388608 | tf_op jit(solution)/shard_map/all_to_all | solution.py:128
  39.6 190.6 %all-gather.3.cloned.1.call-start = ((), (), s32[]{:S(2)}) async-start(), calls=%async_computation.4 | async-start | bytes 4587520 | tf_op jit(solution)/shard_map/all_gather | solution.py:188
  133.1 4.1 %copy-start.8 = (s32[32]{0:T(128)S(1)}, s32[32]{0:T(128)}, u32[]{:S(2)}) copy-start(s32[32]{0:T(128)} %param.19) | copy-start | bytes 388
  133.1 6.7 %copy-start = (bf16[1,64,7168]{2,1,0:T(8,128)(2,1)S(1)}, bf16[1,64,7168]{2,1,0:T(8,128)(2,1)}, u32[]{:S(2)}) copy-start(bf16[1,64,7168]{2,1,0:T(8,128)(2,1)} %param.23) | copy-start | bytes 2752516
  137.2 5.9 %copy-start.7 = (f32[1,7168]{1,0:T(1,128)S(1)}, f32[1,7168]{1,0:T(1,128)}, u32[]{:S(2)}) copy-start(f32[1,7168]{1,0:T(1,128)} %param.21) | copy-start | bytes 86020
  155.1 12.7 %all-to-all-start.3 = ((bf16[32,1,8]{2,1,0:T(2,128)(2,1)}), bf16[32,1,8]{2,1,0:T(2,128)(2,1)S(1)}, u32[]{:S(2)}, u32[]{:S(2)}) async-start(bf16[32,1,8]{2,1,0:T(2,128)(2,1)} %convert_element_type.158), calls=%async_computation.3 | async-start | bytes 32768 | tf_op jit(solution)/shard_map/all_to_all | solution.py:166
  163.9 51.0 %copy-start.5 = (bf16[1,1024,64]{1,2,0:T(8,128)(2,1)S(1)}, bf16[1,1024,64]{1,2,0:T(8,128)(2,1)}, u32[]{:S(2)}) copy-start(bf16[1,1024,64]{1,2,0:T(8,128)(2,1)} %param.25) | copy-start | bytes 393220
  163.9 51.0 %copy-start.6 = (bf16[1,1024,64]{1,2,0:T(8,128)(2,1)S(1)}, bf16[1,1024,64]{1,2,0:T(8,128)(2,1)}, u32[]{:S(2)}) copy-start(bf16[1,1024,64]{1,2,0:T(8,128)(2,1)} %param.24) | copy-start | bytes 393220
  167.9 50.9 %all-to-all-start.2 = ((bf16[32,8,1024]{2,1,0:T(8,128)(2,1)}), bf16[32,8,1024]{2,1,0:T(8,128)(2,1)S(1)}, u32[]{:S(2)}, u32[]{:S(2)}) async-start(bf16[32,8,1024]{2,1,0:T(8,128)(2,1)} %fusion.22), calls=%async_computation.2 | async-start | bytes 1048576 | tf_op jit(solution)/shard_map/all_to_all | solution.py:159
  220.7 12.5 %copy-start.1 = (bf16[1,64,7168]{2,1,0:T(8,128)(2,1)S(1)}, bf16[1,64,7168]{2,1,0:T(8,128)(2,1)}, u32[]{:S(2)}) copy-start(bf16[1,64,7168]{2,1,0:T(8,128)(2,1)} %param.27) | copy-start | bytes 2752516
  220.7 12.5 %copy-start.2 = (bf16[1,64,7168]{2,1,0:T(8,128)(2,1)S(1)}, bf16[1,64,7168]{2,1,0:T(8,128)(2,1)}, u32[]{:S(2)}) copy-start(bf16[1,64,7168]{2,1,0:T(8,128)(2,1)} %param.26) | copy-start | bytes 2752516
Sparse Core Ops, SparseCore 0:
  137.4 92.7 all-gather.2
where the time goes:
time: 244 us
  waiting for transfers between devices  104 us (43%)
  blocking collectives  41.9 us (17%)
  matrix products  25.6 us (10%)
  starting transfers between devices  21.8 us (9%)
  other arithmetic  19.9 us (8%)
  between operations  16.2 us (7%)
  local copies, waits for them, and re-layouts  14.2 us (6%)
    all_to_all x1, waiting for transfers between devices, per_device(): lax.all_to_all(outgoing.reshape(slot_count, capacity, row_width), ('ep',...  91.9 us
    all_gather x1, blocking collectives, per_device(): lax.all_gather(flat_a.astype(jnp.bfloat16), 'ex', axis=0, tiled=True)  41.9 us
    dot_general x1, matrix products, expert_row_block(): jnp.dot(dsc_low, frozen_w.T, preferred_element_type=jnp.float32)  11.3 us
    scatter x1, other arithmetic, per_device(): jnp.zeros((slot_count * capacity, row_width), jnp.bfloat16).at[buffer_row]  9.96 us
    all_gather x1, waiting for transfers between devices, per_device(): lax.all_gather(flat_b.astype(jnp.bfloat16), 'ex', axis=0, tiled=True)  9.41 us
    all_to_all x1, starting transfers between devices, per_device(): lax.all_to_all(outgoing_gate.reshape(slot_count, capacity), ('ep', 'ex'),...  7.3 us
    all_to_all x1, starting transfers between devices, per_device(): lax.all_to_all(outgoing.reshape(slot_count, capacity, row_width), ('ep',...  5.96 us
    all_to_all x1, starting transfers between devices, per_device(): lax.all_to_all(gated_output.reshape(slot_count, capacity), ('ep', 'ex'),...  5.36 us
  transfers between devices with their start and end apart: 5, of which 3 were waited for; matrix products, arithmetic and copies ran while one was open for 17% of the time, Pallas kernels for 0%

commit v1 on v0

v1 whole, which is shorter than its diff:
```python
import functools

import jax
import jax.numpy as jnp
from jax import lax
from jax.experimental import pallas as pl
from jax.experimental.pallas import tpu as pltpu
from jax.sharding import PartitionSpec as P

adapter_scale = 2.0
beta_one = 0.9
beta_two = 0.999
adam_eps = 1e-08
learn_rate = 0.01
weight_decay = 0.01
adam_step = 10

TILE = 512
LANES = 128
SHARES = (5, 6, 3)
VMEM_LIMIT = 24 * 1024 * 1024
EXPERT_VMEM_LIMIT = 44 * 1024 * 1024
bf16 = jnp.bfloat16
f32 = jnp.float32


def chunk_widths(width):
    tiles = width // TILE
    total = sum(SHARES)
    edges = [0]
    taken = 0
    for share in SHARES:
        taken += share
        edges.append(tiles * taken // total)
    return [(edges[i] * TILE, (edges[i + 1] - edges[i]) * TILE) for i in range(len(SHARES)) if edges[i + 1] > edges[i]]


def log2(n):
    k = n.bit_length() - 1
    assert 1 << k == n
    return k


def iota(shape, dim):
    return lax.broadcasted_iota(jnp.int32, shape, dim)


def dot(a, b, ca, cb):
    return lax.dot_general(a, b, (((ca,), (cb,)), ((), ())), preferred_element_type=f32)


HBM = pl.BlockSpec(memory_space=pltpu.HBM)
VMEM = pl.BlockSpec(memory_space=pltpu.VMEM)
SMEM = pl.BlockSpec(memory_space=pltpu.SMEM)
ANY = pl.BlockSpec(memory_space=pl.ANY)
DMA = pltpu.SemaphoreType.DMA


def fetch(pairs, sems):
    copies = [pltpu.make_async_copy(src, dst, sems.at[i]) for i, (src, dst) in enumerate(pairs)]
    for copy in copies:
        copy.start()
    return copies


def call(kernel, outs, flops=0, moved=0, limit=VMEM_LIMIT, **kw):
    params = pltpu.CompilerParams(vmem_limit_bytes=limit)
    cost = pl.CostEstimate(flops=flops, bytes_accessed=moved, transcendentals=0)
    return pl.pallas_call(kernel, out_shape=outs, compiler_params=params, cost_estimate=cost, **kw)


def index_kernel(dims, width, rout_hbm, place_hbm, dout_hbm, hot_ref, chunk_ref, rest_ref, rout_ref, place_ref, sems):
    rest_width = rest_ref.shape[1]
    copies = fetch(
        [
            (rout_hbm, rout_ref),
            (place_hbm, place_ref),
            (dout_hbm.at[:, pl.ds(0, width)], chunk_ref.at[:, pl.ds(0, width)]),
            (dout_hbm.at[:, pl.ds(width, rest_width)], rest_ref),
        ],
        sems,
    )
    copies[0].wait()
    copies[1].wait()
    tok, top, rows, slots, groups, members, cap = dims
    kt = log2(top)
    rid_c, rid_r = iota((rows, 1), 0), iota((1, rows), 1)
    spread = (lax.shift_right_logical(iota((rows, tok), 0), kt) == iota((rows, tok), 1)).astype(bf16)
    routes = rout_ref[...].astype(f32).astype(bf16)
    wide = dot(spread, routes, 1, 1)
    e_col = jnp.sum(jnp.where((iota((rows, top), 0) & (top - 1)) == iota((rows, top), 1), wide, 0.0), axis=1, keepdims=True)
    tall = dot(routes, spread, 1, 1)
    e_row = jnp.sum(jnp.where((iota((top, rows), 1) & (top - 1)) == iota((top, rows), 0), tall, 0.0), axis=0, keepdims=True)
    earlier = rid_r < rid_c
    turn = jnp.sum(jnp.where((e_col == e_row) & earlier, 1.0, 0.0), axis=1, keepdims=True).astype(jnp.int32)
    holds = e_col == place_ref[...].astype(f32)
    slot = iota((rows, slots), 1).astype(f32)
    first = jnp.min(jnp.where(holds, slot, float(slots)), axis=1, keepdims=True)
    last = jnp.max(jnp.where(holds, slot, -1.0), axis=1, keepdims=True)
    target = jnp.where((turn & 1) == 1, last, first)
    target_row = jnp.sum(jnp.where(rid_c == rid_r, target, 0.0), axis=0, keepdims=True)
    pos = jnp.sum(jnp.where((target == target_row) & earlier, 1.0, 0.0), axis=1, keepdims=True).astype(jnp.int32)
    target = target.astype(jnp.int32)
    place = target * cap + pos
    place_z = ((target & (members - 1)) * groups + lax.shift_right_logical(target, log2(members))) * cap + pos
    hot_ref[...] = (place == rid_r).astype(f32).astype(bf16)
    hot_z = (place_z == rid_r).astype(f32).astype(bf16)
    chunk_ref[:, width:] = dot(spread, hot_z, 0, 0).astype(bf16)
    copies[2].wait()
    copies[3].wait()


def tied_kernel(*refs):
    pass


def tied(x, *after):
    return call(
        tied_kernel,
        shape(x.shape),
        in_specs=[ANY] * (1 + len(after)),
        out_specs=ANY,
        input_output_aliases={0: 0},
    )(x, *after)


def hidden_kernel(dims, hot_ref, gate_hbm, hidden_hbm, after_ref, out_ref, gate_ref, hidden_ref, sems):
    tok, top, rows = dims[:3]
    copies = fetch([(gate_hbm, gate_ref), (hidden_hbm, hidden_ref)], sems)
    copies[0].wait()
    width = hidden_ref.shape[1]
    hot = hot_ref[...]
    spread = (lax.shift_right_logical(iota((rows, tok), 0), log2(top)) == iota((rows, tok), 1)).astype(bf16)
    wide = dot(spread, gate_ref[...], 1, 1)
    gate = jnp.sum(jnp.where((iota((rows, top), 0) & (top - 1)) == iota((rows, top), 1), wide, 0.0), axis=1, keepdims=True)
    out_ref[:, width:] = dot(hot, jnp.broadcast_to(gate, (rows, LANES)).astype(bf16), 0, 0).astype(bf16)
    copies[1].wait()
    out_ref[:, :width] = dot(hot, hidden_ref[...], 0, 0).astype(bf16)


def place_direct_kernel(members, *refs):
    out_ref = refs[-1]
    me = lax.axis_index("ex")
    tok = refs[0].shape[0]
    for s in range(members):
        out_ref[pl.ds(pl.multiple_of((me ^ s) * tok, tok), tok), :] = refs[s][...]


def place_relay_kernel(own, near, far, far_near, end, end_near, *refs):
    out_ref = refs[-1]
    me = lax.axis_index("ex")
    tok = own.shape[0]
    orders = (
        (own, near, end, end_near),
        (near, own, far, far_near),
        (far_near, far, own, near),
        (end_near, end, near, own),
    )
    for z, order in enumerate(orders):

        @pl.when(me == z)
        def _():
            for i, ref in enumerate(order):
                out_ref[i * tok : (i + 1) * tok, :] = ref[...]


def pick_kernel(dims, own_ref, other_ref, pick_ref):
    tok, top, rows, slots, groups, members, cap = dims
    tokens = members * tok
    ep, z = lax.axis_index("ep"), lax.axis_index("ex")
    chip, core = lax.shift_right_logical(ep, 1), ep & 1
    row, q = iota((rows, rows), 0), iota((rows, rows), 1)
    p = row & (cap - 1)
    step = lax.shift_right_logical(row, log2(2 * members * cap))
    wanted = (z * groups + (step ^ chip) * 2 + core) * cap + p
    choose = (wanted == q).astype(f32).astype(bf16)
    for b, ref in enumerate((own_ref, other_ref)):
        found = dot(choose, ref[...], 1, 1)
        r = iota((rows, tokens), 0)
        from_core = lax.shift_right_logical(r, log2(members * cap)) & 1
        from_z = lax.shift_right_logical(r, log2(cap)) & (members - 1)
        t = lax.shift_right_logical(iota((rows, tokens), 1), log2(tok))
        keep = (from_core == (core ^ b)) & (from_z == t)
        pick_ref[:, b * tokens : (b + 1) * tokens] = jnp.where(keep, found, 0.0).astype(bf16)


def rows_kernel(start, width, steps, pick_ref, own_ref, other_ref, *out_refs):
    out_refs = out_refs[-steps:]
    tokens = own_ref.shape[0]
    block = out_refs[0].shape[0]
    pick = pick_ref[...]
    for j in range(width // TILE):
        cols = slice(j * TILE, (j + 1) * TILE)
        took = slice(start + j * TILE, start + (j + 1) * TILE)
        got = dot(pick[:, :tokens], own_ref[:, took], 1, 0) + dot(pick[:, tokens:], other_ref[:, took], 1, 0)
        for s, ref in enumerate(out_refs):
            ref[:, cols] = got[s * block : (s + 1) * block].astype(bf16)


def order_by_step(ref, steps, block, cols):
    chip = lax.shift_right_logical(lax.axis_index("ep"), 1)
    return jnp.concatenate(
        [ref[pl.ds(pl.multiple_of((chip ^ s) * block, block), block), cols] for s in range(steps)], axis=0
    )


def low_kernel(steps, block, arrived_ref, down_ref, low_ref, gated_ref):
    hidden = down_ref.shape[1]
    rows = order_by_step(arrived_ref, steps, block, slice(0, hidden))
    gate = order_by_step(arrived_ref, steps, block, slice(hidden, hidden + LANES))[:, :1].astype(f32)
    low = dot(rows, down_ref[...], 1, 1).astype(bf16)
    low_ref[...] = low
    gated_ref[...] = (adapter_scale * gate * low.astype(f32)).astype(bf16)


def up_grad_kernel(steps, *refs):
    blocks, gated_ref, out_ref = refs[:steps], refs[steps], refs[-1]
    for j in range(out_ref.shape[1] // TILE):
        cols = slice(j * TILE, (j + 1) * TILE)
        rows = jnp.concatenate([b[:, cols] for b in blocks], axis=0)
        out_ref[:, cols] = dot(gated_ref[...], rows, 0, 0).astype(bf16)


def expert_kernel(steps, off, unread, first, final, *refs):
    blocks = refs[:steps]
    width = blocks[0].shape[1]
    tiles = width // TILE
    refs = refs[steps:]
    frozen_hbm, scale_hbm, up_hbm = refs[:3]
    refs = refs[3 + unread :]
    frozen_ref, scale_ref, up_ref, sems = refs[-4:]
    refs = refs[:-4]
    copies = fetch(
        [(scale_hbm.at[:, pl.ds(off, width)], scale_ref)]
        + [(frozen_hbm.at[:, pl.ds(off + j * TILE, TILE)], frozen_ref.at[j]) for j in range(tiles)]
        + [(up_hbm.at[:, pl.ds(off, width)], up_ref)],
        sems,
    )
    if not first:
        back_in, low_in = refs[:2]
        refs = refs[2:]
    if final:
        gated_ref, arrived_ref, down_ref, low_ref = refs[:4]
        up_grad_ref, ret_ref, back_ref, thin_ref = refs[4:]
        for j in range(tiles):
            cols = slice(j * TILE, (j + 1) * TILE)
            rows = jnp.concatenate([b[:, cols] for b in blocks], axis=0)
            up_grad_ref[:, cols] = dot(gated_ref[...], rows, 0, 0).astype(bf16)
    else:
        back_ref, thin_ref = refs
    copies[0].wait()
    for j in range(tiles):
        cols = slice(j * TILE, (j + 1) * TILE)
        rows = jnp.concatenate([b[:, cols] for b in blocks], axis=0)
        scaled = (rows.astype(f32) * scale_ref[:, cols]).astype(bf16)
        copies[1 + j].wait()
        part = dot(scaled, frozen_ref[j], 1, 1)
        if j > 0:
            part += back_ref[...]
        elif not first:
            part += back_in[...]
        back_ref[...] = part
    copies[1 + tiles].wait()
    thin = dot(jnp.concatenate([b[...] for b in blocks], axis=0), up_ref[...], 1, 1)
    thin_ref[...] = thin if first else thin + low_in[...]
    if final:
        block = blocks[0].shape[0]
        hidden = down_ref.shape[1]
        chip = lax.shift_right_logical(lax.axis_index("ep"), 1)
        saved = order_by_step(arrived_ref, steps, block, slice(0, hidden))
        gate = order_by_step(arrived_ref, steps, block, slice(hidden, hidden + LANES))[:, :1].astype(f32)
        back = back_ref[...]
        thin = thin_ref[...]
        back_low = (gate * thin).astype(bf16)
        grad = (gate * back + adapter_scale * dot(back_low, down_ref[...], 1, 0)).astype(bf16)
        gate_grad = jnp.sum(saved.astype(f32) * back, axis=1, keepdims=True) + adapter_scale * jnp.sum(
            low_ref[...].astype(f32) * thin, axis=1, keepdims=True
        )
        gate_grad = jnp.broadcast_to(gate_grad, (gate_grad.shape[0], LANES)).astype(bf16)
        for s in range(steps):
            at = pl.ds(pl.multiple_of((chip ^ s) * block, block), block)
            ret_ref[at, :hidden] = grad[s * block : (s + 1) * block]
            ret_ref[at, hidden:] = gate_grad[s * block : (s + 1) * block]
        up_grad_ref[:, width:] = (adapter_scale * dot(back_low, saved, 0, 0)).astype(bf16)


def adam_math(weights, moment, second_moment, gradient):
    weights_wide = weights.astype(f32)
    first = beta_one * moment.astype(f32) + (1.0 - beta_one) * gradient
    second = beta_two * second_moment.astype(f32) + (1.0 - beta_two) * gradient * gradient
    first_hat = first * (1.0 / (1.0 - beta_one**adam_step))
    second_hat = second * (1.0 / (1.0 - beta_two**adam_step))
    fresh = weights_wide - learn_rate * (
        first_hat / (jnp.sqrt(second_hat) + adam_eps) + weight_decay * weights_wide
    )
    return (fresh.astype(bf16), first.astype(bf16), second.astype(bf16))


def pair(partner_ref, members):
    z = lax.axis_index("ex")
    return z, partner_ref[lax.axis_index("ep") * members + z] & (members - 1)


def onward_kernel(members, hop, partner_ref, own_ref, got_ref, *refs):
    out_ref = refs[-1]
    z, mate = pair(partner_ref, members)
    if hop == 2:
        mine = ((z == 1) & (mate >= 2)) | ((z == 2) & (mate <= 1))
    else:
        mine = ((z == 1) & (mate == 0)) | ((z == 2) & (mate == 3))

    @pl.when(mine)
    def _():
        out_ref[...] = own_ref[...]

    @pl.when(jnp.logical_not(mine))
    def _():
        out_ref[...] = got_ref[...]


def adam_kernel(members, parts, unread, partner_ref, own_ref, h1, h2, h3, *refs):
    count = len(parts)
    state, refs = refs[: 3 * count], refs[3 * count + unread :]
    fresh, refs = refs[: 3 * count], refs[3 * count :]
    held, made, in_sems, out_sems = refs
    loads = []
    for n, (at, width, base) in enumerate(parts):
        for k in range(3):
            src = state[3 * n + k].at[:, pl.ds(base, width)]
            loads.append((src, held.at[k, :, pl.ds(at, width)]))
    loads = fetch(loads, in_sems)
    z, mate = pair(partner_ref, members)
    use = (
        ((z == 1) & (mate == 0)) | ((z == 2) & (mate == 3)),
        ((z == 1) & (mate >= 2)) | ((z == 2) & (mate <= 1)),
        ((z == 0) & (mate != 0)) | ((z == 3) & (mate != 3)),
    )
    stores = []
    for n, (at, width, base) in enumerate(parts):
        for load in loads[3 * n : 3 * n + 3]:
            load.wait()
        for j in range(width // TILE):
            cols = slice(at + j * TILE, at + (j + 1) * TILE)
            gradient = own_ref[:, cols].astype(f32)
            for wanted, ref in zip(use, (h1, h2, h3)):
                gradient += jnp.where(wanted, ref[:, cols].astype(f32), 0.0)
            new = adam_math(held[0, :, cols], held[1, :, cols], held[2, :, cols], gradient)
            for k in range(3):
                made[k, :, cols] = new[k]
        for k in range(3):
            dst = fresh[3 * n + k].at[:, pl.ds(base, width)]
            store = pltpu.make_async_copy(made.at[k, :, pl.ds(at, width)], dst, out_sems.at[3 * n + k])
            store.start()
            stores.append(store)
    for store in stores:
        store.wait()


def return_kernel(dims, hot_ref, ret_ref, grad_ref, gate_ref):
    tok, top, rows = dims[:3]
    hidden = grad_ref.shape[1]
    hot = hot_ref[...]
    grad_ref[...] = dot(hot, ret_ref[:, :hidden], 1, 0).astype(bf16)
    gate = dot(hot, ret_ref[:, hidden:], 1, 0)[:, :1]
    spread = jnp.where(lax.shift_right_logical(iota((rows, tok), 0), log2(top)) == iota((rows, tok), 1), gate, 0.0)
    turn = ((iota((top, rows), 1) & (top - 1)) == iota((top, rows), 0)).astype(bf16)
    gate_ref[...] = dot(turn, spread.astype(bf16), 1, 0).astype(bf16)


def shape(dims, dtype=bf16):
    return jax.ShapeDtypeStruct(dims, dtype)


def per_device(
    dout,
    gates,
    saved_down_input,
    routing,
    placement,
    partner,
    frozen,
    colscale,
    adapter_down_factor,
    adapter_up_factor,
    first_moment_down,
    second_moment_down,
    first_moment_up,
    second_moment_up,
):
    groups = lax.axis_size("ep")
    members = lax.axis_size("ex")
    slots = groups * members
    tok, top = routing.shape
    model_width = dout.shape[1]
    hidden = saved_down_input.shape[2]
    rank = adapter_down_factor.shape[2]
    rows = tok * top
    cap = rows // slots
    steps = groups // 2
    block = 2 * members * cap
    dims = (tok, top, rows, slots, groups, members, cap)
    widths = chunk_widths(model_width)
    tokens = members * tok
    assert members == 4 and groups % 2 == 0

    width0 = widths[0][1]
    rest_width = model_width - width0
    hot, chunk0, rest = call(
        functools.partial(index_kernel, dims, width0),
        [shape((rows, rows)), shape((tok, width0 + rows)), shape((tok, rest_width))],
        flops=2 * rows * rows * tok,
        moved=4 * tok * model_width,
        in_specs=[HBM] * 3,
        out_specs=[VMEM] * 3,
        scratch_shapes=[pltpu.VMEM((top, tok), jnp.int32), pltpu.VMEM((1, slots), jnp.int32), DMA((4,))],
    )(routing.T, placement.reshape(1, slots), dout)

    def other_core(x):
        return lax.ppermute(x, "ep", [(i, i ^ 1) for i in range(groups)])

    def send(x, pairs):
        return lax.ppermute(x, "ex", pairs)

    got = [send(chunk0, [(i, i ^ s) for i in range(members)]) for s in range(1, members)]

    rest = tied(rest, *got)
    middle, outer = [(1, 2), (2, 1)], [(1, 0), (2, 3)]
    near = send(rest, [(0, 1), (1, 0), (2, 3), (3, 2)])
    far = send(rest, middle)
    outgoing = call(
        functools.partial(hidden_kernel, dims),
        shape((rows, hidden + LANES)),
        flops=2 * rows * rows * hidden,
        moved=4 * rows * hidden,
        in_specs=[VMEM, HBM, HBM, ANY],
        out_specs=VMEM,
        scratch_shapes=[pltpu.VMEM((top, tok), bf16), pltpu.VMEM((rows, hidden), bf16), DMA((2,))],
    )(hot, gates.T, saved_down_input.reshape(rows, hidden), near)

    arrived = lax.all_to_all(
        outgoing.reshape(slots, cap, hidden + LANES), ("ep", "ex"), split_axis=0, concat_axis=0, tiled=True
    ).reshape(rows, hidden + LANES)

    far_near = send(near, middle)
    end = send(far, outer)
    end_near = send(far_near, outer)

    own0 = call(
        functools.partial(place_direct_kernel, members),
        shape((tokens, width0 + rows)),
        moved=4 * tokens * width0,
    )(chunk0, *got)
    other0 = other_core(own0)
    pick = call(
        functools.partial(pick_kernel, dims),
        shape((rows, rows)),
        flops=2 * rows * rows * 2 * tokens,
        moved=4 * rows * rows,
        grid=(1,),
        in_specs=[pl.BlockSpec((tokens, rows), lambda i: (0, width0 // rows))] * 2,
        out_specs=pl.BlockSpec((rows, rows), lambda i: (0, 0)),
    )(own0, other0)
    down_t = adapter_down_factor[0].T
    low, gated = call(
        functools.partial(low_kernel, steps, block),
        [shape((rows, rank)), shape((rows, rank))],
        flops=2 * rows * hidden * rank,
        moved=2 * rows * hidden,
    )(arrived, down_t)

    def exchange(x, *after):
        h1 = send(x, [(0, 1), (3, 2)])
        hops = [h1]
        for hop, pairs in ((2, middle), (3, outer)):
            onward = call(
                functools.partial(onward_kernel, members, hop),
                shape(x.shape),
                moved=4 * x.size,
                in_specs=[SMEM, VMEM, VMEM] + [ANY] * len(after),
                out_specs=VMEM,
            )(partner, x, hops[-1], *after)
            hops.append(send(onward, pairs))
        return hops

    def plane_rows(c, own, other, start, *after):
        off, width = widths[c]
        blocks = call(
            functools.partial(rows_kernel, start, width, steps),
            [shape((block, width))] * steps,
            flops=2 * rows * rows * width,
            moved=4 * rows * width,
            in_specs=[VMEM] * 3 + [ANY] * len(after),
            out_specs=[VMEM] * steps,
        )(pick, own, other, *after)
        sent = [lax.ppermute(blocks[s], "ep", [(i, i ^ (2 * s)) for i in range(groups)]) for s in range(1, steps)]
        return [blocks[0]] + sent

    def up_grad(blocks, *after):
        out = shape((rank, blocks[0].shape[1]))
        return call(
            functools.partial(up_grad_kernel, steps),
            out,
            flops=2 * rows * rank * out.shape[1],
            in_specs=[VMEM] * (steps + 1) + [ANY] * len(after),
            out_specs=VMEM,
        )(*blocks, gated, *after)

    def expert(c, blocks, after, *carry):
        off, width = widths[c]
        tiles = width // TILE
        final = c == len(widths) - 1
        args = list(blocks) + [frozen[0], colscale, adapter_up_factor[0]] + list(after) + list(carry)
        specs = [VMEM] * steps + [HBM] * 3 + [ANY] * len(after) + [VMEM] * len(carry)
        scratch = []
        if final:
            args += [gated, arrived, down_t, low]
            specs += [VMEM] * 4
            outs = [shape((rank, width + hidden)), shape((rows, hidden + LANES))]
            scratch = [pltpu.VMEM((rows, hidden), f32), pltpu.VMEM((rows, rank), f32)]
        else:
            outs = [shape((rows, hidden), f32), shape((rows, rank), f32)]
        scratch += [
            pltpu.VMEM((tiles, hidden, TILE), bf16),
            pltpu.VMEM((1, width), f32),
            pltpu.VMEM((rank, width), bf16),
            DMA((tiles + 2,)),
        ]
        return call(
            functools.partial(expert_kernel, steps, off, len(after), not carry, final),
            outs,
            flops=2 * rows * hidden * width,
            moved=2 * hidden * width + 2 * rows * width,
            limit=EXPERT_VMEM_LIMIT,
            in_specs=specs,
            out_specs=[VMEM] * len(outs),
            scratch_shapes=scratch,
        )(*args)

    def adam(grad, hops, parts, states, before, *after):
        total = sum(width for _, width, _ in parts)
        arrays = [x for state in states for x in state]
        carried = len(before)
        return call(
            functools.partial(adam_kernel, members, parts, carried + len(after)),
            [shape(x.shape) for x in arrays],
            flops=20 * rank * total,
            moved=20 * rank * total,
            limit=EXPERT_VMEM_LIMIT,
            in_specs=[SMEM] + [VMEM] * 4 + [HBM] * (len(arrays) + carried) + [ANY] * len(after),
            out_specs=[HBM] * len(arrays),
            input_output_aliases={5 + len(arrays) + i: i for i in range(carried)},
            scratch_shapes=[pltpu.VMEM((3, rank, total), bf16)] * 2 + [DMA((len(arrays),))] * 2,
        )(partner, grad, *hops, *arrays, *before, *after)

    up_state = [adapter_up_factor[0], first_moment_up[0], second_moment_up[0]]
    down_state = [down_t, first_moment_down[0].T, second_moment_down[0].T]
    (_, _), (off1, width1), (off2, width2) = widths

    blocks0 = plane_rows(0, own0, other0, 0)
    carry = expert(0, blocks0, [])
    grad0 = up_grad(blocks0)
    own1 = call(
        place_relay_kernel,
        shape((tokens, rest_width)),
        moved=4 * tokens * rest_width,
        in_specs=[VMEM] * 6 + [ANY] * 2,
        out_specs=VMEM,
    )(rest, near, far, far_near, end, end_near, carry[0], grad0)
    other1 = other_core(own1)
    blocks1 = plane_rows(1, own1, other1, 0)
    blocks2 = plane_rows(2, own1, other1, width1, blocks1[0])
    hops0 = exchange(grad0, blocks2[0])
    grad1 = up_grad(blocks1, hops0[1])
    carry = expert(1, blocks1, [blocks2[0]], *carry)
    grad2, ret = expert(2, blocks2, [grad1, hops0[2]], *carry)
    hops1 = exchange(grad1, ret)
    hops2 = exchange(grad2)
    fresh_up = adam(grad0, hops0, [(0, width0, 0)], [up_state], [], ret)
    fresh_up = adam(grad1, hops1, [(0, width1, off1)], [up_state], fresh_up)
    fresh = adam(grad2, hops2, [(0, width2, off2), (width2, hidden, 0)], [up_state, down_state], fresh_up)
    fresh_up, fresh_down = fresh[:3], fresh[3:]

    returned = lax.all_to_all(
        ret.reshape(slots, cap, hidden + LANES), ("ep", "ex"), split_axis=0, concat_axis=0, tiled=True
    ).reshape(rows, hidden + LANES)
    row_grad, gate_grad = call(
        functools.partial(return_kernel, dims),
        [shape((rows, hidden)), shape((top, tok))],
        flops=2 * rows * rows * hidden,
        moved=4 * rows * hidden,
    )(hot, returned)

    return (
        row_grad.reshape(tok, top, hidden),
        gate_grad.T,
        fresh_down[0].T[None],
        fresh_up[0][None],
        fresh_down[1].T[None],
        fresh_down[2].T[None],
        fresh_up[1][None],
        fresh_up[2][None],
    )


def solution(mesh):
    two = P(("ep", "ex"), None)
    three = P(("ep", "ex"), None, None)
    return jax.shard_map(
        per_device,
        mesh=mesh,
        in_specs=(two, two, three, two, P(), P(), three, two) + (three,) * 6,
        out_specs=(three, two) + (three,) * 6,
        check_vma=False,
    )
```

time: 244 us -> 186 us (0.76)
  blocking collectives: 41.9 us -> 0 us
  starting transfers between devices: 21.8 us -> 57.9 us
  Pallas kernels: 0 us -> 35.7 us
  matrix products: 25.6 us -> 0 us
  waiting for transfers between devices: 104 us -> 81.8 us
  other arithmetic: 19.9 us -> 0 us
  between operations: 16.2 us -> 1.21 us
  local copies, waits for them, and re-layouts: 14.2 us -> 8.19 us
    all_to_all x4 -> x2, waiting for transfers between devices: 94.7 us -> 0.01 us  [the longest x1 0.01 us: per_device(): lax.all_to_all(outgoing.reshape(slots, cap, hidden + LANES), ('ep', 'ex')...]
    ppermute x0 -> x28, waiting for transfers between devices: none -> 81.8 us  [the longest x17 54.4 us: send(): return lax.ppermute(x, 'ex', pairs)]
    ppermute x0 -> x28, starting transfers between devices: none -> 48 us  [the longest x17 37.3 us: send(): return lax.ppermute(x, 'ex', pairs)]
    all_gather x1 -> x0, blocking collectives: 41.9 us -> none  [per_device(): lax.all_gather(flat_a.astype(jnp.bfloat16), 'ex', axis=0, tiled=True)]
    pallas_call x0 -> x25, Pallas kernels: none -> 35.7 us  [the longest x3 14.2 us: expert(): call(functools.partial(expert_kernel, steps, off, len(after), not carry,...]
    dot_general x7 -> x0, matrix products: 25.6 us -> none  [the longest x1 11.3 us: expert_row_block(): jnp.dot(dsc_low, frozen_w.T, preferred_element_type=jnp.float32)]
    all_to_all x4 -> x2, starting transfers between devices: 21.6 us -> 9.81 us  [the longest x1 5.01 us: per_device(): lax.all_to_all(outgoing.reshape(slots, cap, hidden + LANES), ('ep', 'ex')...]
    scatter x1 -> x0, other arithmetic: 9.96 us -> none  [per_device(): jnp.zeros((slot_count * capacity, row_width), jnp.bfloat16).at[buffer_row]]
  transfers between devices with their start and end apart: 5 -> 30, of which waited for: 3 -> 13; matrix products, arithmetic and copies ran while one was open for 17% -> 0% of each run, Pallas kernels for 0% -> 17%
where the time goes in v1:
time: 186 us; the launch traced here: 185 us
  waiting for transfers between devices  81.8 us (44%)
  starting transfers between devices  57.9 us (31%)
  Pallas kernels  35.7 us (19%)
  local copies, waits for them, and re-layouts  8.19 us (4%)
    ppermute x17, waiting for transfers between devices, send(): return lax.ppermute(x, 'ex', pairs)  54.4 us
    ppermute x17, starting transfers between devices, send(): return lax.ppermute(x, 'ex', pairs)  37.3 us
    ppermute x9, waiting for transfers between devices, plane_rows(): lax.ppermute(blocks[s], 'ep', [(i, i ^ 2 * s) for i in range(groups)])  27.4 us
    pallas_call x3, Pallas kernels, expert(): call(functools.partial(expert_kernel, steps, off, len(after), not carry,...  14.2 us
    ppermute x9, starting transfers between devices, plane_rows(): lax.ppermute(blocks[s], 'ep', [(i, i ^ 2 * s) for i in range(groups)])  10.6 us
    unnamed x64, local copies, waits for them, and re-layouts  8.19 us
    pallas_call x3, Pallas kernels, adam(): call(functools.partial(adam_kernel, members, parts, carried + len(after))...  8.12 us
    all_to_all x1, starting transfers between devices, per_device(): lax.all_to_all(outgoing.reshape(slots, cap, hidden + LANES), ('ep', 'ex')...  5.01 us
  transfers between devices with their start and end apart: 30, of which 13 were waited for; matrix products, arithmetic and copies ran while one was open for 0% of the time, Pallas kernels for 17%

profile of v1, /device:TPU:0, one launch (start us, length us, event | category | flops | bytes accessed | tf_op | source)
XLA Modules:
  0.0 184.8 jit_solution(9754672316702974719)
XLA Ops:
  4.5 3.1 %collective-permute-start = (bf16[32,2816]{1,0:T(8,128)(2,1)S(1)}, bf16[32,2816]{1,0:T(8,128)(2,1)S(1)}, u32[]{:S(2)}, u32[]{:S(2)}) collective-permute-start(bf16[32,2816]{1,0:T(8,128)(2,1)S(1)} %get-tuple-element.46.refs_0_), channel_id=1, source_target_pairs={{0,1},{1,0},{2,3},{3,2},{4,5},{5,4},{6,7},{7,6},{8,9},{9,8},{10,11... | collective-permute-start | bytes 540680 | tf_op jit(solution)/shard_map/ppermute | solution.py:422
  7.5 2.6 %collective-permute-start.1 = (bf16[32,2816]{1,0:T(8,128)(2,1)S(1)}, bf16[32,2816]{1,0:T(8,128)(2,1)S(1)}, u32[]{:S(2)}, u32[]{:S(2)}) collective-permute-start(bf16[32,2816]{1,0:T(8,128)(2,1)S(1)} %get-tuple-element.46.refs_0_), channel_id=1, source_target_pairs={{0,2},{1,3},{2,0},{3,1},{4,6},{5,7},{6,4},{7,5},{8,10},{9,11},{10,... | collective-permute-start | bytes 540680 | tf_op jit(solution)/shard_map/ppermute | solution.py:422
  10.1 4.9 %collective-permute-done.refs_1_ = bf16[32,2816]{1,0:T(8,128)(2,1)S(1)} collective-permute-done((bf16[32,2816]{1,0:T(8,128)(2,1)S(1)}, bf16[32,2816]{1,0:T(8,128)(2,1)S(1)}, u32[]{:S(2)}, u32[]{:S(2)}) %collective-permute-start) | collective-permute-done | bytes 180256 | tf_op jit(solution)/shard_map/ppermute | solution.py:422
  15.0 8.6 %collective-permute-done.1.refs_2_ = bf16[32,2816]{1,0:T(8,128)(2,1)S(1)} collective-permute-done((bf16[32,2816]{1,0:T(8,128)(2,1)S(1)}, bf16[32,2816]{1,0:T(8,128)(2,1)S(1)}, u32[]{:S(2)}, u32[]{:S(2)}) %collective-permute-start.1) | collective-permute-done | bytes 180256 | tf_op jit(solution)/shard_map/ppermute | solution.py:422
  23.7 3.0 %collective-permute-start.4 = (bf16[32,4608]{1,0:T(8,128)(2,1)}, bf16[32,4608]{1,0:T(8,128)(2,1)S(1)}, u32[]{:S(2)}, u32[]{:S(2)}) collective-permute-start(bf16[32,4608]{1,0:T(8,128)(2,1)} %shard_map.200.own), channel_id=1, source_target_pairs={{0,1},{1,0},{2,3},{3,2},{4,5},{5,4},{6,7},{7,6},{8,9},{9,8},{10,11... | collective-permute-start | bytes 884744 | tf_op jit(solution)/shard_map/ppermute | solution.py:422
  26.8 5.9 %collective-permute-done.4.after_ref.near = bf16[32,4608]{1,0:T(8,128)(2,1)S(1)} collective-permute-done((bf16[32,4608]{1,0:T(8,128)(2,1)}, bf16[32,4608]{1,0:T(8,128)(2,1)S(1)}, u32[]{:S(2)}, u32[]{:S(2)}) %collective-permute-start.4) | collective-permute-done | bytes 294944 | tf_op jit(solution)/shard_map/ppermute | solution.py:422
  34.4 5.0 %all-to-all-start = ((bf16[32,8,1152]{2,1,0:T(8,128)(2,1)}), bf16[32,8,1152]{2,1,0:T(8,128)(2,1)S(1)}, u32[]{:S(2)}, u32[]{:S(2)}) async-start(bf16[32,8,1152]{2,1,0:T(8,128)(2,1)} %bitcast.6), calls=%async_computation | async-start | bytes 1179648 | tf_op jit(solution)/shard_map/all_to_all | solution.py:440
  49.4 14.1 %collective-permute-done.10.refs_2_ = bf16[64,2560]{1,0:T(8,128)(2,1)S(1)} collective-permute-done((bf16[64,2560]{1,0:T(8,128)(2,1)S(1)}, bf16[64,2560]{1,0:T(8,128)(2,1)S(1)}, u32[]{:S(2)}, u32[]{:S(2)}) %collective-permute-start.10) | collective-permute-done | bytes 327712 | tf_op jit(solution)/shard_map/ppermute | solution.py:495
  64.3 4.5 %shard_map.202 = (f32[256,1024]{1,0:T(8,128)S(1)}, f32[256,64]{1,0:T(8,128)S(1)}) custom-call(bf16[64,2560]{1,0:T(8,128)(2,1)S(1)} %get-tuple-element.48.refs_0_, bf16[64,2560]{1,0:T(8,128)(2,1)S(1)} %collective-permute-done.9.refs_1_, bf16[64,2560]{1,0:T(8,128)(2,1)S(1)} %collective-permute-done.10.refs_2_, ...), custom_call_target="tpu_custom_call" | custom-call | flops 1342177280 | bytes 6553600 | tf_op jit(solution)/shard_map/pallas_call | solution.py:528
  79.0 6.6 %collective-permute-start.19 = (bf16[64,2560]{1,0:T(8,128)(2,1)S(1)}, bf16[64,2560]{1,0:T(8,128)(2,1)S(1)}, u32[]{:S(2)}, u32[]{:S(2)}) collective-permute-start(bf16[64,2560]{1,0:T(8,128)(2,1)S(1)} %shard_map.205.refs_1_.own_ref), channel_id=1, source_target_pairs={{0,1},{3,2},{4,5},{7,6},{8,9},{11,10},{12,13},{15,14},{16,17},{19,... | collective-permute-start | bytes 983048 | tf_op jit(solution)/shard_map/ppermute | solution.py:422
  87.2 6.0 %collective-permute-done.19.got_ref.h1 = bf16[64,2560]{1,0:T(8,128)(2,1)S(1)} collective-permute-done((bf16[64,2560]{1,0:T(8,128)(2,1)S(1)}, bf16[64,2560]{1,0:T(8,128)(2,1)S(1)}, u32[]{:S(2)}, u32[]{:S(2)}) %collective-permute-start.19) | collective-permute-done | bytes 327712 | tf_op jit(solution)/shard_map/ppermute | solution.py:422
  101.5 5.1 %collective-permute-done.16.refs_1_ = bf16[64,3072]{1,0:T(8,128)(2,1)S(1)} collective-permute-done((bf16[64,3072]{1,0:T(8,128)(2,1)S(1)}, bf16[64,3072]{1,0:T(8,128)(2,1)S(1)}, u32[]{:S(2)}, u32[]{:S(2)}) %collective-permute-start.16) | collective-permute-done | bytes 393248 | tf_op jit(solution)/shard_map/ppermute | solution.py:495
  108.0 7.0 %collective-permute-done.17.refs_2_ = bf16[64,3072]{1,0:T(8,128)(2,1)S(1)} collective-permute-done((bf16[64,3072]{1,0:T(8,128)(2,1)S(1)}, bf16[64,3072]{1,0:T(8,128)(2,1)S(1)}, u32[]{:S(2)}, u32[]{:S(2)}) %collective-permute-start.17) | collective-permute-done | bytes 393248 | tf_op jit(solution)/shard_map/ppermute | solution.py:495
  116.4 6.9 %collective-permute-start.25 = (bf16[64,3072]{1,0:T(8,128)(2,1)S(1)}, bf16[64,3072]{1,0:T(8,128)(2,1)}, u32[]{:S(2)}, u32[]{:S(2)}) collective-permute-start(bf16[64,3072]{1,0:T(8,128)(2,1)S(1)} %shard_map.210.refs_7_.own_ref), channel_id=1, source_target_pairs={{0,1},{3,2},{4,5},{7,6},{8,9},{11,10},{12,13},{15,14},{16,17},{19,... | collective-permute-start | bytes 1179656 | tf_op jit(solution)/shard_map/ppermute | solution.py:422
  123.3 5.2 %shard_map.212 = (f32[256,1024]{1,0:T(8,128)S(1)}, f32[256,64]{1,0:T(8,128)S(1)}) custom-call(bf16[64,3072]{1,0:T(8,128)(2,1)S(1)} %get-tuple-element.54.out_refs_0_.refs_0_, bf16[64,3072]{1,0:T(8,128)(2,1)S(1)} %collective-permute-done.16.refs_1_, bf16[64,3072]{1,0:T(8,128)(2,1)S(1)} %collective-permute-done.17.refs_2_, ...), custom_call_target="tpu_custom_call" | custom-call | flops 1610612736 | bytes 7864320 | tf_op jit(solution)/shard_map/pallas_call | solution.py:528
  128.6 4.5 %shard_map.213 = (bf16[64,2560]{1,0:T(8,128)(2,1)S(1)}, bf16[256,1152]{1,0:T(8,128)(2,1)}) custom-call(bf16[64,1536]{1,0:T(8,128)(2,1)S(1)} %get-tuple-element.55.refs_0_.refs_7_, bf16[64,1536]{1,0:T(8,128)(2,1)S(1)} %collective-permute-done.13.refs_1_, bf16[64,1536]{1,0:T(8,128)(2,1)S(1)} %collective-permute-done.14.refs_2_, ...), custom_call_target="tpu_custom_call" | custom-call | flops 805306368 | bytes 3932160 | tf_op jit(solution)/shard_map/pallas_call | solution.py:528
  133.1 4.8 %all-to-all-start.1 = ((bf16[32,8,1152]{2,1,0:T(8,128)(2,1)}), bf16[32,8,1152]{2,1,0:T(8,128)(2,1)S(1)}, u32[]{:S(2)}, u32[]{:S(2)}) async-start(bf16[32,8,1152]{2,1,0:T(8,128)(2,1)} %bitcast.10), calls=%async_computation.1 | async-start | bytes 1179648 | tf_op jit(solution)/shard_map/all_to_all | solution.py:583
  137.9 3.7 %collective-permute-start.22 = (bf16[64,2560]{1,0:T(8,128)(2,1)S(1)}, bf16[64,2560]{1,0:T(8,128)(2,1)S(1)}, u32[]{:S(2)}, u32[]{:S(2)}) collective-permute-start(bf16[64,2560]{1,0:T(8,128)(2,1)S(1)} %get-tuple-element.69.own_ref), channel_id=1, source_target_pairs={{0,1},{3,2},{4,5},{7,6},{8,9},{11,10},{12,13},{15,14},{16,17},{19,... | collective-permute-start | bytes 983048 | tf_op jit(solution)/shard_map/ppermute | solution.py:422
  143.4 11.8 %collective-permute-done.22.got_ref.h1 = bf16[64,2560]{1,0:T(8,128)(2,1)S(1)} collective-permute-done((bf16[64,2560]{1,0:T(8,128)(2,1)S(1)}, bf16[64,2560]{1,0:T(8,128)(2,1)S(1)}, u32[]{:S(2)}, u32[]{:S(2)}) %collective-permute-start.22) | collective-permute-done | bytes 327712 | tf_op jit(solution)/shard_map/ppermute | solution.py:422
  160.5 2.5 %shard_map.219 = (bf16[64,7168]{1,0:T(8,128)(2,1)}, bf16[64,7168]{1,0:T(8,128)(2,1)}, bf16[64,7168]{1,0:T(8,128)(2,1)}) custom-call(s32[32]{0:T(128)S(1)} %copy-done.28, bf16[64,2560]{1,0:T(8,128)(2,1)S(1)} %shard_map.205.refs_1_.own_ref, bf16[64,2560]{1,0:T(8,128)(2,1)S(1)} %copy-done.6, bf16[64,2560]{1,0:T(8,128)(2,1)S(1)} %copy-done.4, ...), custom_call_target="tpu_custom_call" | custom-call | flops 3276800 | bytes 3276800 | tf_op jit(solution)/shard_map/pallas_call | solution.py:543
  163.0 12.2 %collective-permute-done.27.h3 = bf16[64,3072]{1,0:T(8,128)(2,1)S(1)} collective-permute-done((bf16[64,3072]{1,0:T(8,128)(2,1)S(1)}, bf16[64,3072]{1,0:T(8,128)(2,1)S(1)}, u32[]{:S(2)}, u32[]{:S(2)}) %collective-permute-start.27) | collective-permute-done | bytes 393248 | tf_op jit(solution)/shard_map/ppermute | solution.py:422
  175.2 3.2 %shard_map.220 = (bf16[64,7168]{1,0:T(8,128)(2,1)}, bf16[64,7168]{1,0:T(8,128)(2,1)}, bf16[64,7168]{1,0:T(8,128)(2,1)}) custom-call(s32[32]{0:T(128)S(1)} %copy-done.28, bf16[64,3072]{1,0:T(8,128)(2,1)S(1)} %shard_map.210.refs_7_.own_ref, ...), custom_call_target="tpu_custom_call", output_to_operand_aliasing={{0}: (8, {}), {1}: (9, {}), {2}: (10, {})} | custom-call | flops 3932160 | bytes 3932160 | tf_op jit(solution)/shard_map/pallas_call | solution.py:543
  178.4 2.7 %collective-permute-done.24.h3 = bf16[64,2560]{1,0:T(8,128)(2,1)S(1)} collective-permute-done((bf16[64,2560]{1,0:T(8,128)(2,1)S(1)}, bf16[64,2560]{1,0:T(8,128)(2,1)S(1)}, u32[]{:S(2)}, u32[]{:S(2)}) %collective-permute-start.24) | collective-permute-done | bytes 327712 | tf_op jit(solution)/shard_map/ppermute | solution.py:422
  181.1 2.4 %shard_map.221 = (bf16[64,7168]{1,0:T(8,128)(2,1)}, bf16[64,7168]{1,0:T(8,128)(2,1)}, bf16[64,7168]{1,0:T(8,128)(2,1)}, bf16[64,1024]{1,0:T(8,128)(2,1)}, bf16[6...) custom-call(s32[32]{0:T(128)S(1)} %copy-done.28, ...), custom_call_target="tpu_custom_call", output_to_operand_aliasing={{0}: (11, {}), {1}: (12, {}), {2}: (13, {})} | custom-call | flops 3276800 | bytes 3276800 | tf_op jit(solution)/shard_map/pallas_call | solution.py:543
  (125 shorter events, 47.2 us)
Async XLA Ops:
  4.5 10.6 %collective-permute-start = (bf16[32,2816]{1,0:T(8,128)(2,1)S(1)}, bf16[32,2816]{1,0:T(8,128)(2,1)S(1)}, u32[]{:S(2)}, u32[]{:S(2)}) collective-permute-start(bf16[32,2816]{1,0:T(8,128)(2,1)S(1)} %get-tuple-element.46.refs_0_), channel_id=1, source_target_pairs={{0,1},{1,0},{2,3},{3,2},{4,5},{5,4},{6,7},{7,6},{8,9},{9,8},{10,11... | collective-permute-start | bytes 540680 | tf_op jit(solution)/shard_map/ppermute | solution.py:422
  7.5 16.1 %collective-permute-start.1 = (bf16[32,2816]{1,0:T(8,128)(2,1)S(1)}, bf16[32,2816]{1,0:T(8,128)(2,1)S(1)}, u32[]{:S(2)}, u32[]{:S(2)}) collective-permute-start(bf16[32,2816]{1,0:T(8,128)(2,1)S(1)} %get-tuple-element.46.refs_0_), channel_id=1, source_target_pairs={{0,2},{1,3},{2,0},{3,1},{4,6},{5,7},{6,4},{7,5},{8,10},{9,11},{10,... | collective-permute-start | bytes 540680 | tf_op jit(solution)/shard_map/ppermute | solution.py:422
  10.1 13.5 %collective-permute-start.2 = (bf16[32,2816]{1,0:T(8,128)(2,1)S(1)}, bf16[32,2816]{1,0:T(8,128)(2,1)S(1)}, u32[]{:S(2)}, u32[]{:S(2)}) collective-permute-start(bf16[32,2816]{1,0:T(8,128)(2,1)S(1)} %get-tuple-element.46.refs_0_), channel_id=1, source_target_pairs={{0,3},{1,2},{2,1},{3,0},{4,7},{5,6},{6,5},{7,4},{8,11},{9,10},{10,... | collective-permute-start | bytes 540680 | tf_op jit(solution)/shard_map/ppermute | solution.py:422
  26.7 15.4 %collective-permute-start.3 = (bf16[128,2816]{1,0:T(8,128)(2,1)S(1)}, bf16[128,2816]{1,0:T(8,128)(2,1)S(1)}, u32[]{:S(2)}, u32[]{:S(2)}) collective-permute-start(bf16[128,2816]{1,0:T(8,128)(2,1)S(1)} %shard_map.198.own_ref), channel_id=1, source_target_pairs={{0,4},{4,0},{8,12},{12,8},{16,20},{20,16},{24,28},{28,24},{1,5},{5... | collective-permute-start | bytes 2162696 | tf_op jit(solution)/shard_map/ppermute | solution.py:419
  34.4 37.3 %all-to-all-start = ((bf16[32,8,1152]{2,1,0:T(8,128)(2,1)}), bf16[32,8,1152]{2,1,0:T(8,128)(2,1)S(1)}, u32[]{:S(2)}, u32[]{:S(2)}) async-start(bf16[32,8,1152]{2,1,0:T(8,128)(2,1)} %bitcast.6), calls=%async_computation | async-start | bytes 1179648 | tf_op jit(solution)/shard_map/all_to_all | solution.py:440
  43.3 20.2 %collective-permute-start.10 = (bf16[64,2560]{1,0:T(8,128)(2,1)S(1)}, bf16[64,2560]{1,0:T(8,128)(2,1)S(1)}, u32[]{:S(2)}, u32[]{:S(2)}) collective-permute-start(bf16[64,2560]{1,0:T(8,128)(2,1)S(1)} %get-tuple-element.50), channel_id=1, source_target_pairs={{0,16},{4,20},{8,24},{12,28},{16,0},{20,4},{24,8},{28,12},{1,17},{... | collective-permute-start | bytes 983048 | tf_op jit(solution)/shard_map/ppermute | solution.py:495
  45.1 18.4 %collective-permute-start.11 = (bf16[64,2560]{1,0:T(8,128)(2,1)S(1)}, bf16[64,2560]{1,0:T(8,128)(2,1)S(1)}, u32[]{:S(2)}, u32[]{:S(2)}) collective-permute-start(bf16[64,2560]{1,0:T(8,128)(2,1)S(1)} %get-tuple-element.51), channel_id=1, source_target_pairs={{0,24},{4,28},{8,16},{12,20},{16,8},{20,12},{24,0},{28,4},{1,25},{... | collective-permute-start | bytes 983048 | tf_op jit(solution)/shard_map/ppermute | solution.py:495
  46.6 17.8 %collective-permute-start.9 = (bf16[64,2560]{1,0:T(8,128)(2,1)S(1)}, bf16[64,2560]{1,0:T(8,128)(2,1)S(1)}, u32[]{:S(2)}, u32[]{:S(2)}) collective-permute-start(bf16[64,2560]{1,0:T(8,128)(2,1)S(1)} %get-tuple-element.49), channel_id=1, source_target_pairs={{0,8},{4,12},{8,0},{12,4},{16,24},{20,28},{24,16},{28,20},{1,9},{5... | collective-permute-start | bytes 983048 | tf_op jit(solution)/shard_map/ppermute | solution.py:495
  46.8 28.5 %collective-permute-start.7 = (bf16[32,4608]{1,0:T(8,128)(2,1)}, bf16[32,4608]{1,0:T(8,128)(2,1)}, u32[]{:S(2)}, u32[]{:S(2)}) collective-permute-start(bf16[32,4608]{1,0:T(8,128)(2,1)} %collective-permute-done.5.far), channel_id=1, source_target_pairs={{1,0},{2,3},{5,4},{6,7},{9,8},{10,11},{13,12},{14,15},{17,16},{18,... | collective-permute-start | bytes 884744 | tf_op jit(solution)/shard_map/ppermute | solution.py:422
  48.1 29.4 %collective-permute-start.8 = (bf16[32,4608]{1,0:T(8,128)(2,1)}, bf16[32,4608]{1,0:T(8,128)(2,1)}, u32[]{:S(2)}, u32[]{:S(2)}) collective-permute-start(bf16[32,4608]{1,0:T(8,128)(2,1)} %collective-permute-done.6.far_near), channel_id=1, source_target_pairs={{1,0},{2,3},{5,4},{6,7},{9,8},{10,11},{13,12},{14,15},{17,16},{18,... | collective-permute-start | bytes 884744 | tf_op jit(solution)/shard_map/ppermute | solution.py:422
  79.0 14.2 %collective-permute-start.19 = (bf16[64,2560]{1,0:T(8,128)(2,1)S(1)}, bf16[64,2560]{1,0:T(8,128)(2,1)S(1)}, u32[]{:S(2)}, u32[]{:S(2)}) collective-permute-start(bf16[64,2560]{1,0:T(8,128)(2,1)S(1)} %shard_map.205.refs_1_.own_ref), channel_id=1, source_target_pairs={{0,1},{3,2},{4,5},{7,6},{8,9},{11,10},{12,13},{15,14},{16,17},{19,... | collective-permute-start | bytes 983048 | tf_op jit(solution)/shard_map/ppermute | solution.py:422
  94.5 12.1 %collective-permute-start.16 = (bf16[64,3072]{1,0:T(8,128)(2,1)S(1)}, bf16[64,3072]{1,0:T(8,128)(2,1)S(1)}, u32[]{:S(2)}, u32[]{:S(2)}) collective-permute-start(bf16[64,3072]{1,0:T(8,128)(2,1)S(1)} %get-tuple-element.59), channel_id=1, source_target_pairs={{0,8},{4,12},{8,0},{12,4},{16,24},{20,28},{24,16},{28,20},{1,9},{5... | collective-permute-start | bytes 1179656 | tf_op jit(solution)/shard_map/ppermute | solution.py:495
  96.0 19.0 %collective-permute-start.17 = (bf16[64,3072]{1,0:T(8,128)(2,1)S(1)}, bf16[64,3072]{1,0:T(8,128)(2,1)S(1)}, u32[]{:S(2)}, u32[]{:S(2)}) collective-permute-start(bf16[64,3072]{1,0:T(8,128)(2,1)S(1)} %get-tuple-element.60), channel_id=1, source_target_pairs={{0,16},{4,20},{8,24},{12,28},{16,0},{20,4},{24,8},{28,12},{1,17},{... | collective-permute-start | bytes 1179656 | tf_op jit(solution)/shard_map/ppermute | solution.py:495
  97.5 18.4 %collective-permute-start.18 = (bf16[64,3072]{1,0:T(8,128)(2,1)S(1)}, bf16[64,3072]{1,0:T(8,128)(2,1)S(1)}, u32[]{:S(2)}, u32[]{:S(2)}) collective-permute-start(bf16[64,3072]{1,0:T(8,128)(2,1)S(1)} %get-tuple-element.61), channel_id=1, source_target_pairs={{0,24},{4,28},{8,16},{12,20},{16,8},{20,12},{24,0},{28,4},{1,25},{... | collective-permute-start | bytes 1179656 | tf_op jit(solution)/shard_map/ppermute | solution.py:495
  98.6 29.9 %collective-permute-start.21 = (bf16[64,2560]{1,0:T(8,128)(2,1)S(1)}, bf16[64,2560]{1,0:T(8,128)(2,1)S(1)}, u32[]{:S(2)}, u32[]{:S(2)}) collective-permute-start(bf16[64,2560]{1,0:T(8,128)(2,1)S(1)} %shard_map.211), channel_id=1, source_target_pairs={{1,0},{2,3},{5,4},{6,7},{9,8},{10,11},{13,12},{14,15},{17,16},{18,... | collective-permute-start | bytes 983048 | tf_op jit(solution)/shard_map/ppermute | solution.py:422
  99.9 28.6 %collective-permute-start.13 = (bf16[64,1536]{1,0:T(8,128)(2,1)S(1)}, bf16[64,1536]{1,0:T(8,128)(2,1)S(1)}, u32[]{:S(2)}, u32[]{:S(2)}) collective-permute-start(bf16[64,1536]{1,0:T(8,128)(2,1)S(1)} %get-tuple-element.56), channel_id=1, source_target_pairs={{0,8},{4,12},{8,0},{12,4},{16,24},{20,28},{24,16},{28,20},{1,9},{5... | collective-permute-start | bytes 589832 | tf_op jit(solution)/shard_map/ppermute | solution.py:495
  106.6 22.0 %collective-permute-start.14 = (bf16[64,1536]{1,0:T(8,128)(2,1)S(1)}, bf16[64,1536]{1,0:T(8,128)(2,1)S(1)}, u32[]{:S(2)}, u32[]{:S(2)}) collective-permute-start(bf16[64,1536]{1,0:T(8,128)(2,1)S(1)} %get-tuple-element.57), channel_id=1, source_target_pairs={{0,16},{4,20},{8,24},{12,28},{16,0},{20,4},{24,8},{28,12},{1,17},{... | collective-permute-start | bytes 589832 | tf_op jit(solution)/shard_map/ppermute | solution.py:495
  115.0 13.5 %collective-permute-start.15 = (bf16[64,1536]{1,0:T(8,128)(2,1)S(1)}, bf16[64,1536]{1,0:T(8,128)(2,1)S(1)}, u32[]{:S(2)}, u32[]{:S(2)}) collective-permute-start(bf16[64,1536]{1,0:T(8,128)(2,1)S(1)} %get-tuple-element.58), channel_id=1, source_target_pairs={{0,24},{4,28},{8,16},{12,20},{16,8},{20,12},{24,0},{28,4},{1,25},{... | collective-permute-start | bytes 589832 | tf_op jit(solution)/shard_map/ppermute | solution.py:495
  116.4 25.3 %collective-permute-start.25 = (bf16[64,3072]{1,0:T(8,128)(2,1)S(1)}, bf16[64,3072]{1,0:T(8,128)(2,1)}, u32[]{:S(2)}, u32[]{:S(2)}) collective-permute-start(bf16[64,3072]{1,0:T(8,128)(2,1)S(1)} %shard_map.210.refs_7_.own_ref), channel_id=1, source_target_pairs={{0,1},{3,2},{4,5},{7,6},{8,9},{11,10},{12,13},{15,14},{16,17},{19,... | collective-permute-start | bytes 1179656 | tf_op jit(solution)/shard_map/ppermute | solution.py:422
  133.1 50.5 %all-to-all-start.1 = ((bf16[32,8,1152]{2,1,0:T(8,128)(2,1)}), bf16[32,8,1152]{2,1,0:T(8,128)(2,1)S(1)}, u32[]{:S(2)}, u32[]{:S(2)}) async-start(bf16[32,8,1152]{2,1,0:T(8,128)(2,1)} %bitcast.10), calls=%async_computation.1 | async-start | bytes 1179648 | tf_op jit(solution)/shard_map/all_to_all | solution.py:583
  137.9 17.2 %collective-permute-start.22 = (bf16[64,2560]{1,0:T(8,128)(2,1)S(1)}, bf16[64,2560]{1,0:T(8,128)(2,1)S(1)}, u32[]{:S(2)}, u32[]{:S(2)}) collective-permute-start(bf16[64,2560]{1,0:T(8,128)(2,1)S(1)} %get-tuple-element.69.own_ref), channel_id=1, source_target_pairs={{0,1},{3,2},{4,5},{7,6},{8,9},{11,10},{12,13},{15,14},{16,17},{19,... | collective-permute-start | bytes 983048 | tf_op jit(solution)/shard_map/ppermute | solution.py:422
  142.7 13.9 %collective-permute-start.26 = (bf16[64,3072]{1,0:T(8,128)(2,1)S(1)}, bf16[64,3072]{1,0:T(8,128)(2,1)S(1)}, u32[]{:S(2)}, u32[]{:S(2)}) collective-permute-start(bf16[64,3072]{1,0:T(8,128)(2,1)S(1)} %shard_map.217), channel_id=1, source_target_pairs={{1,2},{2,1},{5,6},{6,5},{9,10},{10,9},{13,14},{14,13},{17,18},{18,... | collective-permute-start | bytes 1179656 | tf_op jit(solution)/shard_map/ppermute | solution.py:422
  157.2 17.9 %collective-permute-start.27 = (bf16[64,3072]{1,0:T(8,128)(2,1)S(1)}, bf16[64,3072]{1,0:T(8,128)(2,1)S(1)}, u32[]{:S(2)}, u32[]{:S(2)}) collective-permute-start(bf16[64,3072]{1,0:T(8,128)(2,1)S(1)} %shard_map.218), channel_id=1, source_target_pairs={{1,0},{2,3},{5,4},{6,7},{9,8},{10,11},{13,12},{14,15},{17,16},{18,... | collective-permute-start | bytes 1179656 | tf_op jit(solution)/shard_map/ppermute | solution.py:422
  159.1 22.0 %collective-permute-start.24 = (bf16[64,2560]{1,0:T(8,128)(2,1)S(1)}, bf16[64,2560]{1,0:T(8,128)(2,1)S(1)}, u32[]{:S(2)}, u32[]{:S(2)}) collective-permute-start(bf16[64,2560]{1,0:T(8,128)(2,1)S(1)} %shard_map.216), channel_id=1, source_target_pairs={{1,0},{2,3},{5,4},{6,7},{9,8},{10,11},{13,12},{14,15},{17,16},{18,... | collective-permute-start | bytes 983048 | tf_op jit(solution)/shard_map/ppermute | solution.py:422
  (38 other events, 247.0 us)

commit v2 on v1

--- a/solution.py
+++ b/solution.py
@@ -427,20 +427,6 @@
     middle, outer = [(1, 2), (2, 1)], [(1, 0), (2, 3)]
     near = send(rest, [(0, 1), (1, 0), (2, 3), (3, 2)])
     far = send(rest, middle)
-    outgoing = call(
-        functools.partial(hidden_kernel, dims),
-        shape((rows, hidden + LANES)),
-        flops=2 * rows * rows * hidden,
-        moved=4 * rows * hidden,
-        in_specs=[VMEM, HBM, HBM, ANY],
-        out_specs=VMEM,
-        scratch_shapes=[pltpu.VMEM((top, tok), bf16), pltpu.VMEM((rows, hidden), bf16), DMA((2,))],
-    )(hot, gates.T, saved_down_input.reshape(rows, hidden), near)
-
-    arrived = lax.all_to_all(
-        outgoing.reshape(slots, cap, hidden + LANES), ("ep", "ex"), split_axis=0, concat_axis=0, tiled=True
-    ).reshape(rows, hidden + LANES)
-
     far_near = send(near, middle)
     end = send(far, outer)
     end_near = send(far_near, outer)
@@ -461,26 +447,19 @@
         out_specs=pl.BlockSpec((rows, rows), lambda i: (0, 0)),
     )(own0, other0)
     down_t = adapter_down_factor[0].T
-    low, gated = call(
-        functools.partial(low_kernel, steps, block),
-        [shape((rows, rank)), shape((rows, rank))],
-        flops=2 * rows * hidden * rank,
-        moved=2 * rows * hidden,
-    )(arrived, down_t)
-
-    def exchange(x, *after):
-        h1 = send(x, [(0, 1), (3, 2)])
-        hops = [h1]
-        for hop, pairs in ((2, middle), (3, outer)):
-            onward = call(
-                functools.partial(onward_kernel, members, hop),
-                shape(x.shape),
-                moved=4 * x.size,
-                in_specs=[SMEM, VMEM, VMEM] + [ANY] * len(after),
-                out_specs=VMEM,
-            )(partner, x, hops[-1], *after)
-            hops.append(send(onward, pairs))
-        return hops
+
+    def onward(hop, x, got, *after):
+        moved = call(
+            functools.partial(onward_kernel, members, hop),
+            shape(x.shape),
+            moved=4 * x.size,
+            in_specs=[SMEM, VMEM, VMEM] + [ANY] * len(after),
+            out_specs=VMEM,
+        )(partner, x, got, *after)
+        return send(moved, middle if hop == 2 else outer)
+
+    def first_hop(x):
+        return send(x, [(0, 1), (3, 2)])
 
     def plane_rows(c, own, other, start, *after):
         off, width = widths[c]
@@ -557,38 +536,70 @@
     (_, _), (off1, width1), (off2, width2) = widths
 
     blocks0 = plane_rows(0, own0, other0, 0)
-    carry = expert(0, blocks0, [])
-    grad0 = up_grad(blocks0)
+    outgoing = call(
+        functools.partial(hidden_kernel, dims),
+        shape((rows, hidden + LANES)),
+        flops=2 * rows * rows * hidden,
+        moved=4 * rows * hidden,
+        in_specs=[VMEM, HBM, HBM, ANY],
+        out_specs=VMEM,
+        scratch_shapes=[pltpu.VMEM((top, tok), bf16), pltpu.VMEM((rows, hidden), bf16), DMA((2,))],
+    )(hot, gates.T, saved_down_input.reshape(rows, hidden), blocks0[0])
+
+    arrived = lax.all_to_all(
+        outgoing.reshape(slots, cap, hidden + LANES), ("ep", "ex"), split_axis=0, concat_axis=0, tiled=True
+    ).reshape(rows, hidden + LANES)
+
+    low, gated = call(
+        functools.partial(low_kernel, steps, block),
+        [shape((rows, rank)), shape((rows, rank))],
+        flops=2 * rows * hidden * rank,
+        moved=2 * rows * hidden,
+    )(arrived, down_t)
+
     own1 = call(
         place_relay_kernel,
         shape((tokens, rest_width)),
         moved=4 * tokens * rest_width,
-        in_specs=[VMEM] * 6 + [ANY] * 2,
+        in_specs=[VMEM] * 6 + [ANY] * steps,
         out_specs=VMEM,
-    )(rest, near, far, far_near, end, end_near, carry[0], grad0)
+    )(rest, near, far, far_near, end, end_near, outgoing, *blocks0[1:])
     other1 = other_core(own1)
     blocks1 = plane_rows(1, own1, other1, 0)
     blocks2 = plane_rows(2, own1, other1, width1, blocks1[0])
-    hops0 = exchange(grad0, blocks2[0])
-    grad1 = up_grad(blocks1, hops0[1])
-    carry = expert(1, blocks1, [blocks2[0]], *carry)
-    grad2, ret = expert(2, blocks2, [grad1, hops0[2]], *carry)
-    hops1 = exchange(grad1, ret)
-    hops2 = exchange(grad2)
-    fresh_up = adam(grad0, hops0, [(0, width0, 0)], [up_state], [], ret)
-    fresh_up = adam(grad1, hops1, [(0, width1, off1)], [up_state], fresh_up)
-    fresh = adam(grad2, hops2, [(0, width2, off2), (width2, hidden, 0)], [up_state, down_state], fresh_up)
-    fresh_up, fresh_down = fresh[:3], fresh[3:]
-
+    grad0 = up_grad(blocks0, blocks2[0])
+    carry0 = expert(0, blocks0, [grad0])
+    grad1 = up_grad(blocks1, carry0[0])
+    first0 = first_hop(grad0)
+    first1 = first_hop(grad1)
+    second0 = onward(2, grad0, first0, grad1)
+    carry1 = expert(1, blocks1, [grad1], *carry0)
+    grad2, ret = expert(2, blocks2, [carry1[0], second0, first1], *carry1)
+    third0 = onward(3, grad0, second0, carry1[0])
+    second1 = onward(2, grad1, first1, carry1[0])
+    first2 = first_hop(grad2)
     returned = lax.all_to_all(
         ret.reshape(slots, cap, hidden + LANES), ("ep", "ex"), split_axis=0, concat_axis=0, tiled=True
     ).reshape(rows, hidden + LANES)
+    third1 = onward(3, grad1, second1, ret)
+    fresh_up = adam(grad0, (first0, second0, third0), [(0, width0, 0)], [up_state], [], ret)
+    second2 = onward(2, grad2, first2, ret)
     row_grad, gate_grad = call(
         functools.partial(return_kernel, dims),
         [shape((rows, hidden)), shape((top, tok))],
         flops=2 * rows * rows * hidden,
         moved=4 * rows * hidden,
     )(hot, returned)
+    third2 = onward(3, grad2, second2, row_grad, fresh_up[0])
+    fresh_up = adam(grad1, (first1, second1, third1), [(0, width1, off1)], [up_state], fresh_up)
+    fresh = adam(
+        grad2,
+        (first2, second2, third2),
+        [(0, width2, off2), (width2, hidden, 0)],
+        [up_state, down_state],
+        fresh_up,
+    )
+    fresh_up, fresh_down = fresh[:3], fresh[3:]
 
     return (
         row_grad.reshape(tok, top, hidden),

time: 186 us -> 167 us (0.90)
  waiting for transfers between devices: 81.8 us -> 66.4 us
  starting transfers between devices: 57.9 us -> 47 us
  Pallas kernels: 35.7 us -> 40.4 us
  local copies, waits for them, and re-layouts: 8.19 us -> 10.4 us
    ppermute x9, waiting for transfers between devices: 27.4 us -> 1.1 us  [plane_rows(): lax.ppermute(blocks[s], 'ep', [(i, i ^ 2 * s) for i in range(groups)])]
    all_to_all x1, waiting for transfers between devices: 0.01 us -> 9.47 us  [per_device(): lax.all_to_all(outgoing.reshape(slots, cap, hidden + LANES), ('ep', 'ex')...]
    ppermute x17, starting transfers between devices: 37.3 us -> 28.3 us  [send(): return lax.ppermute(x, 'ex', pairs)]
    unnamed x64 -> x92, local copies, waits for them, and re-layouts: 8.19 us -> 10.4 us
  transfers between devices with their start and end apart: 30 -> 30, of which waited for: 13 -> 10; matrix products, arithmetic and copies ran while one was open for 0% -> 0% of each run, Pallas kernels for 17% -> 19%
where the time goes in v2:
time: 167 us; the launch traced here: 166 us
  waiting for transfers between devices  66.4 us (40%)
  starting transfers between devices  47 us (28%)
  Pallas kernels  40.4 us (24%)
  local copies, waits for them, and re-layouts  10.4 us (6%)
    ppermute x17, waiting for transfers between devices, send(): return lax.ppermute(x, 'ex', pairs)  55.8 us
    ppermute x17, starting transfers between devices, send(): return lax.ppermute(x, 'ex', pairs)  28.3 us
    pallas_call x3, Pallas kernels, expert(): call(functools.partial(expert_kernel, steps, off, len(after), not carry,...  15.6 us
    ppermute x9, starting transfers between devices, plane_rows(): lax.ppermute(blocks[s], 'ep', [(i, i ^ 2 * s) for i in range(groups)])  10.6 us
    unnamed x92, local copies, waits for them, and re-layouts  10.4 us
    all_to_all x1, waiting for transfers between devices, per_device(): lax.all_to_all(outgoing.reshape(slots, cap, hidden + LANES), ('ep', 'ex')...  9.47 us
    pallas_call x3, Pallas kernels, adam(): call(functools.partial(adam_kernel, members, parts, carried + len(after))...  8.6 us
    pallas_call x6, Pallas kernels, onward(): call(functools.partial(onward_kernel, members, hop), shape(x.shape), move...  5.52 us
  transfers between devices with their start and end apart: 30, of which 10 were waited for; matrix products, arithmetic and copies ran while one was open for 0% of the time, Pallas kernels for 19%

profile of v2, /device:TPU:0, one launch (start us, length us, event | category | flops | bytes accessed | tf_op | source)
XLA Modules:
  0.0 165.8 jit_solution(18395219018736414175)
XLA Ops:
  3.7 5.1 %collective-permute-start.2 = (bf16[32,2816]{1,0:T(8,128)(2,1)S(1)}, bf16[32,2816]{1,0:T(8,128)(2,1)S(1)}, u32[]{:S(2)}, u32[]{:S(2)}) collective-permute-start(bf16[32,2816]{1,0:T(8,128)(2,1)S(1)} %get-tuple-element.46.refs_0_), channel_id=1, source_target_pairs={{0,3},{1,2},{2,1},{3,0},{4,7},{5,6},{6,5},{7,4},{8,11},{9,10},{10,... | collective-permute-start | bytes 540680 | tf_op jit(solution)/shard_map/ppermute | solution.py:422
  9.5 4.9 %collective-permute-done.2.refs_3_ = bf16[32,2816]{1,0:T(8,128)(2,1)S(1)} collective-permute-done((bf16[32,2816]{1,0:T(8,128)(2,1)S(1)}, bf16[32,2816]{1,0:T(8,128)(2,1)S(1)}, u32[]{:S(2)}, u32[]{:S(2)}) %collective-permute-start.2) | collective-permute-done | bytes 180256 | tf_op jit(solution)/shard_map/ppermute | solution.py:422
  14.4 9.8 %collective-permute-done.1.refs_2_ = bf16[32,2816]{1,0:T(8,128)(2,1)S(1)} collective-permute-done((bf16[32,2816]{1,0:T(8,128)(2,1)S(1)}, bf16[32,2816]{1,0:T(8,128)(2,1)S(1)}, u32[]{:S(2)}, u32[]{:S(2)}) %collective-permute-start.1) | collective-permute-done | bytes 180256 | tf_op jit(solution)/shard_map/ppermute | solution.py:422
  25.1 8.6 %collective-permute-done.4.near = bf16[32,4608]{1,0:T(8,128)(2,1)S(1)} collective-permute-done((bf16[32,4608]{1,0:T(8,128)(2,1)S(1)}, bf16[32,4608]{1,0:T(8,128)(2,1)S(1)}, u32[]{:S(2)}, u32[]{:S(2)}) %collective-permute-start.4) | collective-permute-done | bytes 294944 | tf_op jit(solution)/shard_map/ppermute | solution.py:422
  43.3 8.0 %collective-permute-done.7.end = bf16[32,4608]{1,0:T(8,128)(2,1)S(1)} collective-permute-done((bf16[32,4608]{1,0:T(8,128)(2,1)S(1)}, bf16[32,4608]{1,0:T(8,128)(2,1)S(1)}, u32[]{:S(2)}, u32[]{:S(2)}) %collective-permute-start.7) | collective-permute-done | bytes 294944 | tf_op jit(solution)/shard_map/ppermute | solution.py:422
  51.3 4.3 %collective-permute-done.8.end_near = bf16[32,4608]{1,0:T(8,128)(2,1)S(1)} collective-permute-done((bf16[32,4608]{1,0:T(8,128)(2,1)S(1)}, bf16[32,4608]{1,0:T(8,128)(2,1)S(1)}, u32[]{:S(2)}, u32[]{:S(2)}) %collective-permute-start.8) | collective-permute-done | bytes 294944 | tf_op jit(solution)/shard_map/ppermute | solution.py:422
  56.6 4.2 %all-to-all-start = ((bf16[32,8,1152]{2,1,0:T(8,128)(2,1)}), bf16[32,8,1152]{2,1,0:T(8,128)(2,1)S(1)}, u32[]{:S(2)}, u32[]{:S(2)}) async-start(bf16[32,8,1152]{2,1,0:T(8,128)(2,1)} %bitcast.6), calls=%async_computation | async-start | bytes 1179648 | tf_op jit(solution)/shard_map/all_to_all | solution.py:549
  60.8 1.9 %shard_map.204 = (bf16[64,3072]{1,0:T(8,128)(2,1)S(1)}, bf16[64,3072]{1,0:T(8,128)(2,1)}, bf16[64,3072]{1,0:T(8,128)(2,1)}, bf16[64,3072]{1,0:T(8,128)(2,1)}) custom-call(bf16[256,256]{1,0:T(8,128)(2,1)S(1)} %shard_map.199.pick_ref, bf16[128,4608]{1,0:T(8,128)(2,1)S(1)} %shard_map.203.own_ref, bf16[128,4608]{1,0:T(8,128)(2,1)S(1)} %collective-permute-done.12.other_ref), custom_call_target="tpu_custom_call" | custom-call | flops 402653184 | bytes 3145728 | tf_op jit(solution)/shard_map/pallas_call | solution.py:466
  63.5 1.8 %collective-permute-start.16 = (bf16[64,3072]{1,0:T(8,128)(2,1)}, bf16[64,3072]{1,0:T(8,128)(2,1)}, u32[]{:S(2)}, u32[]{:S(2)}) collective-permute-start(bf16[64,3072]{1,0:T(8,128)(2,1)} %get-tuple-element.57), channel_id=1, source_target_pairs={{0,8},{4,12},{8,0},{12,4},{16,24},{20,28},{24,16},{28,20},{1,9},{5... | collective-permute-start | bytes 1179656 | tf_op jit(solution)/shard_map/ppermute | solution.py:474
  67.0 9.5 %all-to-all-done = bf16[32,8,1152]{2,1,0:T(8,128)(2,1)S(1)} async-done(((bf16[32,8,1152]{2,1,0:T(8,128)(2,1)}), bf16[32,8,1152]{2,1,0:T(8,128)(2,1)S(1)}, u32[]{:S(2)}, u32[]{:S(2)}) %all-to-all-start) | async-done | bytes 589856 | tf_op jit(solution)/shard_map/all_to_all | solution.py:549
  79.4 4.6 %collective-permute-start.19 = (bf16[64,2560]{1,0:T(8,128)(2,1)S(1)}, bf16[64,2560]{1,0:T(8,128)(2,1)S(1)}, u32[]{:S(2)}, u32[]{:S(2)}) collective-permute-start(bf16[64,2560]{1,0:T(8,128)(2,1)S(1)} %shard_map.207.refs_7_.own_ref), channel_id=1, source_target_pairs={{0,1},{3,2},{4,5},{7,6},{8,9},{11,10},{12,13},{15,14},{16,17},{19,... | collective-permute-start | bytes 983048 | tf_op jit(solution)/shard_map/ppermute | solution.py:422
  84.0 4.5 %shard_map.208 = (f32[256,1024]{1,0:T(8,128)S(1)}, f32[256,64]{1,0:T(8,128)S(1)}) custom-call(bf16[64,2560]{1,0:T(8,128)(2,1)S(1)} %copy-done.26, bf16[64,2560]{1,0:T(8,128)(2,1)S(1)} %copy-done.20, bf16[64,2560]{1,0:T(8,128)(2,1)S(1)} %copy-done.22, bf16[64,2560]{1,0:T(8,128)(2,1)S(1)} %copy-done.24, bf16[1024,7168]{1,0:T(8,128)(2,1)} %bitcast.60, ...), custom_call_target="tpu_custom_call" | custom-call | flops 1342177280 | bytes 6553600 | tf_op jit(solution)/shard_map/pallas_call | solution.py:507
  90.3 3.2 %collective-permute-start.21 = (bf16[64,3072]{1,0:T(8,128)(2,1)S(1)}, bf16[64,3072]{1,0:T(8,128)(2,1)S(1)}, u32[]{:S(2)}, u32[]{:S(2)}) collective-permute-start(bf16[64,3072]{1,0:T(8,128)(2,1)S(1)} %shard_map.209.refs_7_.refs_0_.own_ref), channel_id=1, source_target_pairs={{0,1},{3,2},{4,5},{7,6},{8,9},{11,10},{12,13},{15,14},{16,17},{19,... | collective-permute-start | bytes 1179656 | tf_op jit(solution)/shard_map/ppermute | solution.py:422
  98.5 6.4 %shard_map.210 = (f32[256,1024]{1,0:T(8,128)S(1)}, f32[256,64]{1,0:T(8,128)S(1)}) custom-call(bf16[64,3072]{1,0:T(8,128)(2,1)S(1)} %copy-done.11, bf16[64,3072]{1,0:T(8,128)(2,1)} %collective-permute-done.16.refs_1_, bf16[64,3072]{1,0:T(8,128)(2,1)} %collective-permute-done.17.refs_2_, bf16[64,3072]{1,0:T(8,128)(2,1)} %collective-permute-done.18.refs_3_, ...), custom_call_target="tpu_custom_call" | custom-call | flops 1610612736 | bytes 7864320 | tf_op jit(solution)/shard_map/pallas_call | solution.py:507
  106.1 4.6 %shard_map.212 = (bf16[64,2560]{1,0:T(8,128)(2,1)S(1)}, bf16[256,1152]{1,0:T(8,128)(2,1)}) custom-call(bf16[64,1536]{1,0:T(8,128)(2,1)S(1)} %get-tuple-element.53.refs_5_.refs_0_, bf16[64,1536]{1,0:T(8,128)(2,1)S(1)} %collective-permute-done.13.refs_1_, bf16[64,1536]{1,0:T(8,128)(2,1)S(1)} %collective-permute-done.14.refs_2_, ...), custom_call_target="tpu_custom_call" | custom-call | flops 805306368 | bytes 3932160 | tf_op jit(solution)/shard_map/pallas_call | solution.py:507
  111.5 3.8 %all-to-all-start.1 = ((bf16[32,8,1152]{2,1,0:T(8,128)(2,1)}), bf16[32,8,1152]{2,1,0:T(8,128)(2,1)}, u32[]{:S(2)}, u32[]{:S(2)}) async-start(bf16[32,8,1152]{2,1,0:T(8,128)(2,1)} %bitcast.10), calls=%async_computation.1 | async-start | bytes 1179648 | tf_op jit(solution)/shard_map/all_to_all | solution.py:581
  115.3 3.8 %collective-permute-start.22 = (bf16[64,2560]{1,0:T(8,128)(2,1)S(1)}, bf16[64,2560]{1,0:T(8,128)(2,1)S(1)}, u32[]{:S(2)}, u32[]{:S(2)}) collective-permute-start(bf16[64,2560]{1,0:T(8,128)(2,1)S(1)} %copy-done.13), channel_id=1, source_target_pairs={{0,1},{3,2},{4,5},{7,6},{8,9},{11,10},{12,13},{15,14},{16,17},{19,... | collective-permute-start | bytes 983048 | tf_op jit(solution)/shard_map/ppermute | solution.py:422
  122.4 10.0 %collective-permute-done.22.got_ref.h1 = bf16[64,2560]{1,0:T(8,128)(2,1)S(1)} collective-permute-done((bf16[64,2560]{1,0:T(8,128)(2,1)S(1)}, bf16[64,2560]{1,0:T(8,128)(2,1)S(1)}, u32[]{:S(2)}, u32[]{:S(2)}) %collective-permute-start.22) | collective-permute-done | bytes 327712 | tf_op jit(solution)/shard_map/ppermute | solution.py:422
  138.8 2.5 %shard_map.216 = (bf16[64,7168]{1,0:T(8,128)(2,1)}, bf16[64,7168]{1,0:T(8,128)(2,1)}, bf16[64,7168]{1,0:T(8,128)(2,1)}) custom-call(s32[32]{0:T(128)S(1)} %copy-done.42, bf16[64,2560]{1,0:T(8,128)(2,1)S(1)} %copy-done.5, bf16[64,2560]{1,0:T(8,128)(2,1)S(1)} %copy-done.32, bf16[64,2560]{1,0:T(8,128)(2,1)S(1)} %copy-done.18, ...), custom_call_target="tpu_custom_call" | custom-call | flops 3276800 | bytes 3276800 | tf_op jit(solution)/shard_map/pallas_call | solution.py:522
  141.2 2.3 %shard_map.213 = (bf16[256,1024]{1,0:T(8,128)(2,1)}, bf16[8,32]{1,0:T(8,128)(2,1)}) custom-call(bf16[256,256]{1,0:T(8,128)(2,1)S(1)} %copy-done.36, bf16[256,1152]{1,0:T(8,128)(2,1)} %bitcast.11.ret_ref), custom_call_target="tpu_custom_call" | custom-call | flops 134217728 | bytes 1048576 | tf_op jit(solution)/shard_map/pallas_call | solution.py:587
  149.2 4.1 %collective-permute-done.27.h3 = bf16[64,3072]{1,0:T(8,128)(2,1)} collective-permute-done((bf16[64,3072]{1,0:T(8,128)(2,1)}, bf16[64,3072]{1,0:T(8,128)(2,1)}, u32[]{:S(2)}, u32[]{:S(2)}) %collective-permute-start.27) | collective-permute-done | bytes 393248 | tf_op jit(solution)/shard_map/ppermute | solution.py:422
  153.3 3.3 %shard_map.220 = (bf16[64,7168]{1,0:T(8,128)(2,1)}, bf16[64,7168]{1,0:T(8,128)(2,1)}, bf16[64,7168]{1,0:T(8,128)(2,1)}) custom-call(s32[32]{0:T(128)S(1)} %copy-done.42, bf16[64,3072]{1,0:T(8,128)(2,1)S(1)} %shard_map.209.refs_7_.refs_0_.own_ref, bf16[64,3072]{1,0:T(8,128)(2,1)S(1)} %copy-done.8, ...), custom_call_target="tpu_custom_call", output_to_operand_aliasing={{0}: (8, {}), {1}: (9, {}), {2}: (10, {})} | custom-call | flops 3932160 | bytes 3932160 | tf_op jit(solution)/shard_map/pallas_call | solution.py:522
  156.5 6.2 %collective-permute-done.25.h3 = bf16[64,2560]{1,0:T(8,128)(2,1)S(1)} collective-permute-done((bf16[64,2560]{1,0:T(8,128)(2,1)S(1)}, bf16[64,2560]{1,0:T(8,128)(2,1)S(1)}, u32[]{:S(2)}, u32[]{:S(2)}) %collective-permute-start.25) | collective-permute-done | bytes 327712 | tf_op jit(solution)/shard_map/ppermute | solution.py:422
  162.7 2.9 %shard_map.221 = (bf16[64,7168]{1,0:T(8,128)(2,1)}, bf16[64,7168]{1,0:T(8,128)(2,1)}, bf16[64,7168]{1,0:T(8,128)(2,1)}, bf16[64,1024]{1,0:T(8,128)(2,1)}, bf16[6...) custom-call(s32[32]{0:T(128)S(1)} %copy-done.42, ...), custom_call_target="tpu_custom_call", output_to_operand_aliasing={{0}: (11, {}), {1}: (12, {}), {2}: (13, {})} | custom-call | flops 3276800 | bytes 3276800 | tf_op jit(solution)/shard_map/pallas_call | solution.py:522
  (153 shorter events, 44.1 us)
Async XLA Ops:
  3.7 10.6 %collective-permute-start.2 = (bf16[32,2816]{1,0:T(8,128)(2,1)S(1)}, bf16[32,2816]{1,0:T(8,128)(2,1)S(1)}, u32[]{:S(2)}, u32[]{:S(2)}) collective-permute-start(bf16[32,2816]{1,0:T(8,128)(2,1)S(1)} %get-tuple-element.46.refs_0_), channel_id=1, source_target_pairs={{0,3},{1,2},{2,1},{3,0},{4,7},{5,6},{6,5},{7,4},{8,11},{9,10},{10,... | collective-permute-start | bytes 540680 | tf_op jit(solution)/shard_map/ppermute | solution.py:422
  8.9 15.3 %collective-permute-start.1 = (bf16[32,2816]{1,0:T(8,128)(2,1)S(1)}, bf16[32,2816]{1,0:T(8,128)(2,1)S(1)}, u32[]{:S(2)}, u32[]{:S(2)}) collective-permute-start(bf16[32,2816]{1,0:T(8,128)(2,1)S(1)} %get-tuple-element.46.refs_0_), channel_id=1, source_target_pairs={{0,2},{1,3},{2,0},{3,1},{4,6},{5,7},{6,4},{7,5},{8,10},{9,11},{10,... | collective-permute-start | bytes 540680 | tf_op jit(solution)/shard_map/ppermute | solution.py:422
  8.9 15.3 %collective-permute-start = (bf16[32,2816]{1,0:T(8,128)(2,1)S(1)}, bf16[32,2816]{1,0:T(8,128)(2,1)S(1)}, u32[]{:S(2)}, u32[]{:S(2)}) collective-permute-start(bf16[32,2816]{1,0:T(8,128)(2,1)S(1)} %get-tuple-element.46.refs_0_), channel_id=1, source_target_pairs={{0,1},{1,0},{2,3},{3,2},{4,5},{5,4},{6,7},{7,6},{8,9},{9,8},{10,11... | collective-permute-start | bytes 540680 | tf_op jit(solution)/shard_map/ppermute | solution.py:422
  24.2 10.2 %collective-permute-start.3 = (bf16[128,2816]{1,0:T(8,128)(2,1)S(1)}, bf16[128,2816]{1,0:T(8,128)(2,1)S(1)}, u32[]{:S(2)}, u32[]{:S(2)}) collective-permute-start(bf16[128,2816]{1,0:T(8,128)(2,1)S(1)} %shard_map.198.own_ref), channel_id=1, source_target_pairs={{0,4},{4,0},{8,12},{12,8},{16,20},{20,16},{24,28},{28,24},{1,5},{5... | collective-permute-start | bytes 2162696 | tf_op jit(solution)/shard_map/ppermute | solution.py:419
  24.4 14.7 %collective-permute-start.5 = (bf16[32,4608]{1,0:T(8,128)(2,1)S(1)}, bf16[32,4608]{1,0:T(8,128)(2,1)S(1)}, u32[]{:S(2)}, u32[]{:S(2)}) collective-permute-start(bf16[32,4608]{1,0:T(8,128)(2,1)S(1)} %shard_map.200.own), channel_id=1, source_target_pairs={{1,2},{2,1},{5,6},{6,5},{9,10},{10,9},{13,14},{14,13},{17,18},{18,... | collective-permute-start | bytes 884744 | tf_op jit(solution)/shard_map/ppermute | solution.py:422
  35.5 20.1 %collective-permute-start.9 = (bf16[64,2560]{1,0:T(8,128)(2,1)S(1)}, bf16[64,2560]{1,0:T(8,128)(2,1)S(1)}, u32[]{:S(2)}, u32[]{:S(2)}) collective-permute-start(bf16[64,2560]{1,0:T(8,128)(2,1)S(1)} %get-tuple-element.49), channel_id=1, source_target_pairs={{0,8},{4,12},{8,0},{12,4},{16,24},{20,28},{24,16},{28,20},{1,9},{5... | collective-permute-start | bytes 983048 | tf_op jit(solution)/shard_map/ppermute | solution.py:474
  37.1 18.6 %collective-permute-start.10 = (bf16[64,2560]{1,0:T(8,128)(2,1)S(1)}, bf16[64,2560]{1,0:T(8,128)(2,1)S(1)}, u32[]{:S(2)}, u32[]{:S(2)}) collective-permute-start(bf16[64,2560]{1,0:T(8,128)(2,1)S(1)} %get-tuple-element.50), channel_id=1, source_target_pairs={{0,16},{4,20},{8,24},{12,28},{16,0},{20,4},{24,8},{28,12},{1,17},{... | collective-permute-start | bytes 983048 | tf_op jit(solution)/shard_map/ppermute | solution.py:474
  38.6 17.1 %collective-permute-start.11 = (bf16[64,2560]{1,0:T(8,128)(2,1)S(1)}, bf16[64,2560]{1,0:T(8,128)(2,1)S(1)}, u32[]{:S(2)}, u32[]{:S(2)}) collective-permute-start(bf16[64,2560]{1,0:T(8,128)(2,1)S(1)} %get-tuple-element.51), channel_id=1, source_target_pairs={{0,24},{4,28},{8,16},{12,20},{16,8},{20,12},{24,0},{28,4},{1,25},{... | collective-permute-start | bytes 983048 | tf_op jit(solution)/shard_map/ppermute | solution.py:474
  39.1 12.3 %collective-permute-start.7 = (bf16[32,4608]{1,0:T(8,128)(2,1)S(1)}, bf16[32,4608]{1,0:T(8,128)(2,1)S(1)}, u32[]{:S(2)}, u32[]{:S(2)}) collective-permute-start(bf16[32,4608]{1,0:T(8,128)(2,1)S(1)} %collective-permute-done.5.far), channel_id=1, source_target_pairs={{1,0},{2,3},{5,4},{6,7},{9,8},{10,11},{13,12},{14,15},{17,16},{18,... | collective-permute-start | bytes 884744 | tf_op jit(solution)/shard_map/ppermute | solution.py:422
  40.4 15.3 %collective-permute-start.8 = (bf16[32,4608]{1,0:T(8,128)(2,1)S(1)}, bf16[32,4608]{1,0:T(8,128)(2,1)S(1)}, u32[]{:S(2)}, u32[]{:S(2)}) collective-permute-start(bf16[32,4608]{1,0:T(8,128)(2,1)S(1)} %collective-permute-done.6.far_near), channel_id=1, source_target_pairs={{1,0},{2,3},{5,4},{6,7},{9,8},{10,11},{13,12},{14,15},{17,16},{18,... | collective-permute-start | bytes 884744 | tf_op jit(solution)/shard_map/ppermute | solution.py:422
  56.6 19.9 %all-to-all-start = ((bf16[32,8,1152]{2,1,0:T(8,128)(2,1)}), bf16[32,8,1152]{2,1,0:T(8,128)(2,1)S(1)}, u32[]{:S(2)}, u32[]{:S(2)}) async-start(bf16[32,8,1152]{2,1,0:T(8,128)(2,1)} %bitcast.6), calls=%async_computation | async-start | bytes 1179648 | tf_op jit(solution)/shard_map/all_to_all | solution.py:549
  63.5 25.1 %collective-permute-start.16 = (bf16[64,3072]{1,0:T(8,128)(2,1)}, bf16[64,3072]{1,0:T(8,128)(2,1)}, u32[]{:S(2)}, u32[]{:S(2)}) collective-permute-start(bf16[64,3072]{1,0:T(8,128)(2,1)} %get-tuple-element.57), channel_id=1, source_target_pairs={{0,8},{4,12},{8,0},{12,4},{16,24},{20,28},{24,16},{28,20},{1,9},{5... | collective-permute-start | bytes 1179656 | tf_op jit(solution)/shard_map/ppermute | solution.py:474
  65.3 23.3 %collective-permute-start.17 = (bf16[64,3072]{1,0:T(8,128)(2,1)}, bf16[64,3072]{1,0:T(8,128)(2,1)}, u32[]{:S(2)}, u32[]{:S(2)}) collective-permute-start(bf16[64,3072]{1,0:T(8,128)(2,1)} %get-tuple-element.58), channel_id=1, source_target_pairs={{0,16},{4,20},{8,24},{12,28},{16,0},{20,4},{24,8},{28,12},{1,17},{... | collective-permute-start | bytes 1179656 | tf_op jit(solution)/shard_map/ppermute | solution.py:474
  66.8 21.9 %collective-permute-start.18 = (bf16[64,3072]{1,0:T(8,128)(2,1)}, bf16[64,3072]{1,0:T(8,128)(2,1)}, u32[]{:S(2)}, u32[]{:S(2)}) collective-permute-start(bf16[64,3072]{1,0:T(8,128)(2,1)} %get-tuple-element.59), channel_id=1, source_target_pairs={{0,24},{4,28},{8,16},{12,20},{16,8},{20,12},{24,0},{28,4},{1,25},{... | collective-permute-start | bytes 1179656 | tf_op jit(solution)/shard_map/ppermute | solution.py:474
  79.4 14.0 %collective-permute-start.19 = (bf16[64,2560]{1,0:T(8,128)(2,1)S(1)}, bf16[64,2560]{1,0:T(8,128)(2,1)S(1)}, u32[]{:S(2)}, u32[]{:S(2)}) collective-permute-start(bf16[64,2560]{1,0:T(8,128)(2,1)S(1)} %shard_map.207.refs_7_.own_ref), channel_id=1, source_target_pairs={{0,1},{3,2},{4,5},{7,6},{8,9},{11,10},{12,13},{15,14},{16,17},{19,... | collective-permute-start | bytes 983048 | tf_op jit(solution)/shard_map/ppermute | solution.py:422
  90.3 15.8 %collective-permute-start.21 = (bf16[64,3072]{1,0:T(8,128)(2,1)S(1)}, bf16[64,3072]{1,0:T(8,128)(2,1)S(1)}, u32[]{:S(2)}, u32[]{:S(2)}) collective-permute-start(bf16[64,3072]{1,0:T(8,128)(2,1)S(1)} %shard_map.209.refs_7_.refs_0_.own_ref), channel_id=1, source_target_pairs={{0,1},{3,2},{4,5},{7,6},{8,9},{11,10},{12,13},{15,14},{16,17},{19,... | collective-permute-start | bytes 1179656 | tf_op jit(solution)/shard_map/ppermute | solution.py:422
  94.1 12.0 %collective-permute-start.20 = (bf16[64,2560]{1,0:T(8,128)(2,1)S(1)}, bf16[64,2560]{1,0:T(8,128)(2,1)S(1)}, u32[]{:S(2)}, u32[]{:S(2)}) collective-permute-start(bf16[64,2560]{1,0:T(8,128)(2,1)S(1)} %shard_map.211), channel_id=1, source_target_pairs={{1,2},{2,1},{5,6},{6,5},{9,10},{10,9},{13,14},{14,13},{17,18},{18,... | collective-permute-start | bytes 983048 | tf_op jit(solution)/shard_map/ppermute | solution.py:422
  96.0 10.0 %collective-permute-start.14 = (bf16[64,1536]{1,0:T(8,128)(2,1)S(1)}, bf16[64,1536]{1,0:T(8,128)(2,1)S(1)}, u32[]{:S(2)}, u32[]{:S(2)}) collective-permute-start(bf16[64,1536]{1,0:T(8,128)(2,1)S(1)} %get-tuple-element.55), channel_id=1, source_target_pairs={{0,16},{4,20},{8,24},{12,28},{16,0},{20,4},{24,8},{28,12},{1,17},{... | collective-permute-start | bytes 589832 | tf_op jit(solution)/shard_map/ppermute | solution.py:474
  111.5 29.7 %all-to-all-start.1 = ((bf16[32,8,1152]{2,1,0:T(8,128)(2,1)}), bf16[32,8,1152]{2,1,0:T(8,128)(2,1)}, u32[]{:S(2)}, u32[]{:S(2)}) async-start(bf16[32,8,1152]{2,1,0:T(8,128)(2,1)} %bitcast.10), calls=%async_computation.1 | async-start | bytes 1179648 | tf_op jit(solution)/shard_map/all_to_all | solution.py:581
  115.3 17.1 %collective-permute-start.22 = (bf16[64,2560]{1,0:T(8,128)(2,1)S(1)}, bf16[64,2560]{1,0:T(8,128)(2,1)S(1)}, u32[]{:S(2)}, u32[]{:S(2)}) collective-permute-start(bf16[64,2560]{1,0:T(8,128)(2,1)S(1)} %copy-done.13), channel_id=1, source_target_pairs={{0,1},{3,2},{4,5},{7,6},{8,9},{11,10},{12,13},{15,14},{16,17},{19,... | collective-permute-start | bytes 983048 | tf_op jit(solution)/shard_map/ppermute | solution.py:422
  119.7 15.6 %collective-permute-start.26 = (bf16[64,3072]{1,0:T(8,128)(2,1)S(1)}, bf16[64,3072]{1,0:T(8,128)(2,1)S(1)}, u32[]{:S(2)}, u32[]{:S(2)}) collective-permute-start(bf16[64,3072]{1,0:T(8,128)(2,1)S(1)} %shard_map.218), channel_id=1, source_target_pairs={{1,2},{2,1},{5,6},{6,5},{9,10},{10,9},{13,14},{14,13},{17,18},{18,... | collective-permute-start | bytes 1179656 | tf_op jit(solution)/shard_map/ppermute | solution.py:422
  121.1 17.5 %collective-permute-start.24 = (bf16[64,2560]{1,0:T(8,128)(2,1)S(1)}, bf16[64,2560]{1,0:T(8,128)(2,1)S(1)}, u32[]{:S(2)}, u32[]{:S(2)}) collective-permute-start(bf16[64,2560]{1,0:T(8,128)(2,1)S(1)} %shard_map.215), channel_id=1, source_target_pairs={{1,0},{2,3},{5,4},{6,7},{9,8},{10,11},{13,12},{14,15},{17,16},{18,... | collective-permute-start | bytes 983048 | tf_op jit(solution)/shard_map/ppermute | solution.py:422
  137.4 15.8 %collective-permute-start.27 = (bf16[64,3072]{1,0:T(8,128)(2,1)}, bf16[64,3072]{1,0:T(8,128)(2,1)}, u32[]{:S(2)}, u32[]{:S(2)}) collective-permute-start(bf16[64,3072]{1,0:T(8,128)(2,1)} %shard_map.219), channel_id=1, source_target_pairs={{1,0},{2,3},{5,4},{6,7},{9,8},{10,11},{13,12},{14,15},{17,16},{18,... | collective-permute-start | bytes 1179656 | tf_op jit(solution)/shard_map/ppermute | solution.py:422
  147.9 14.9 %collective-permute-start.25 = (bf16[64,2560]{1,0:T(8,128)(2,1)S(1)}, bf16[64,2560]{1,0:T(8,128)(2,1)S(1)}, u32[]{:S(2)}, u32[]{:S(2)}) collective-permute-start(bf16[64,2560]{1,0:T(8,128)(2,1)S(1)} %shard_map.217), channel_id=1, source_target_pairs={{1,0},{2,3},{5,4},{6,7},{9,8},{10,11},{13,12},{14,15},{17,16},{18,... | collective-permute-start | bytes 983048 | tf_op jit(solution)/shard_map/ppermute | solution.py:422
  (52 other events, 343.8 us)

commit v3 on v2

--- a/solution.py
+++ b/solution.py
@@ -19,7 +19,7 @@
 LANES = 128
 SHARES = (5, 6, 3)
 VMEM_LIMIT = 24 * 1024 * 1024
-EXPERT_VMEM_LIMIT = 44 * 1024 * 1024
+EXPERT_VMEM_LIMIT = 42 * 1024 * 1024
 bf16 = jnp.bfloat16
 f32 = jnp.float32
 
@@ -456,7 +456,7 @@
             in_specs=[SMEM, VMEM, VMEM] + [ANY] * len(after),
             out_specs=VMEM,
         )(partner, x, got, *after)
-        return send(moved, middle if hop == 2 else outer)
+        return moved, send(moved, middle if hop == 2 else outer)
 
     def first_hop(x):
         return send(x, [(0, 1), (3, 2)])
@@ -572,25 +572,25 @@
     grad1 = up_grad(blocks1, carry0[0])
     first0 = first_hop(grad0)
     first1 = first_hop(grad1)
-    second0 = onward(2, grad0, first0, grad1)
+    msecond0, second0 = onward(2, grad0, first0, grad1)
     carry1 = expert(1, blocks1, [grad1], *carry0)
-    grad2, ret = expert(2, blocks2, [carry1[0], second0, first1], *carry1)
-    third0 = onward(3, grad0, second0, carry1[0])
-    second1 = onward(2, grad1, first1, carry1[0])
+    mthird0, third0 = onward(3, grad0, second0, carry1[0])
+    msecond1, second1 = onward(2, grad1, first1, carry1[0])
+    grad2, ret = expert(2, blocks2, [carry1[0], mthird0, first1], *carry1)
     first2 = first_hop(grad2)
     returned = lax.all_to_all(
         ret.reshape(slots, cap, hidden + LANES), ("ep", "ex"), split_axis=0, concat_axis=0, tiled=True
     ).reshape(rows, hidden + LANES)
-    third1 = onward(3, grad1, second1, ret)
+    mthird1, third1 = onward(3, grad1, second1, ret)
     fresh_up = adam(grad0, (first0, second0, third0), [(0, width0, 0)], [up_state], [], ret)
-    second2 = onward(2, grad2, first2, ret)
+    msecond2, second2 = onward(2, grad2, first2, ret)
     row_grad, gate_grad = call(
         functools.partial(return_kernel, dims),
         [shape((rows, hidden)), shape((top, tok))],
         flops=2 * rows * rows * hidden,
         moved=4 * rows * hidden,
     )(hot, returned)
-    third2 = onward(3, grad2, second2, row_grad, fresh_up[0])
+    mthird2, third2 = onward(3, grad2, second2, fresh_up[0])
     fresh_up = adam(grad1, (first1, second1, third1), [(0, width1, off1)], [up_state], fresh_up)
     fresh = adam(
         grad2,

time: 167 us -> 164 us (0.982)
  waiting for transfers between devices: 66.4 us -> 70.3 us
  Pallas kernels: 40.4 us -> 37.5 us
  local copies, waits for them, and re-layouts: 10.4 us -> 7.6 us
    ppermute x17, waiting for transfers between devices: 55.8 us -> 60.6 us  [send(): return lax.ppermute(x, 'ex', pairs)]
    unnamed x92 -> x74, local copies, waits for them, and re-layouts: 10.4 us -> 7.6 us
    pallas_call x6, Pallas kernels: 5.52 us -> 3.69 us  [onward(): call(functools.partial(onward_kernel, members, hop), shape(x.shape), move...]
  transfers between devices with their start and end apart: 30 -> 30, of which waited for: 10 -> 10; matrix products, arithmetic and copies ran while one was open for 0% -> 0% of each run, Pallas kernels for 19% -> 18%
where the time goes in v3:
time: 164 us; the launch traced here: 163 us
  waiting for transfers between devices  70.3 us (43%)
  starting transfers between devices  46 us (28%)
  Pallas kernels  37.5 us (23%)
  local copies, waits for them, and re-layouts  7.6 us (5%)
    ppermute x17, waiting for transfers between devices, send(): return lax.ppermute(x, 'ex', pairs)  60.6 us
    ppermute x17, starting transfers between devices, send(): return lax.ppermute(x, 'ex', pairs)  27.3 us
    pallas_call x3, Pallas kernels, expert(): call(functools.partial(expert_kernel, steps, off, len(after), not carry,...  15.5 us
    ppermute x9, starting transfers between devices, plane_rows(): lax.ppermute(blocks[s], 'ep', [(i, i ^ 2 * s) for i in range(groups)])  10.6 us
    all_to_all x1, waiting for transfers between devices, per_device(): lax.all_to_all(outgoing.reshape(slots, cap, hidden + LANES), ('ep', 'ex')...  9.46 us
    pallas_call x3, Pallas kernels, adam(): call(functools.partial(adam_kernel, members, parts, carried + len(after))...  7.61 us
    unnamed x74, local copies, waits for them, and re-layouts  7.6 us
    all_to_all x1, starting transfers between devices, per_device(): lax.all_to_all(outgoing.reshape(slots, cap, hidden + LANES), ('ep', 'ex')...  4.2 us
  transfers between devices with their start and end apart: 30, of which 10 were waited for; matrix products, arithmetic and copies ran while one was open for 0% of the time, Pallas kernels for 18%

profile of v3, /device:TPU:0, one launch (start us, length us, event | category | flops | bytes accessed | tf_op | source)
XLA Modules:
  0.0 162.8 jit_solution(13732672377698911501)
XLA Ops:
  3.7 5.1 %collective-permute-start.2 = (bf16[32,2816]{1,0:T(8,128)(2,1)S(1)}, bf16[32,2816]{1,0:T(8,128)(2,1)S(1)}, u32[]{:S(2)}, u32[]{:S(2)}) collective-permute-start(bf16[32,2816]{1,0:T(8,128)(2,1)S(1)} %get-tuple-element.46.refs_0_), channel_id=1, source_target_pairs={{0,3},{1,2},{2,1},{3,0},{4,7},{5,6},{6,5},{7,4},{8,11},{9,10},{10,... | collective-permute-start | bytes 540680 | tf_op jit(solution)/shard_map/ppermute | solution.py:422
  9.5 4.9 %collective-permute-done.2.refs_3_ = bf16[32,2816]{1,0:T(8,128)(2,1)S(1)} collective-permute-done((bf16[32,2816]{1,0:T(8,128)(2,1)S(1)}, bf16[32,2816]{1,0:T(8,128)(2,1)S(1)}, u32[]{:S(2)}, u32[]{:S(2)}) %collective-permute-start.2) | collective-permute-done | bytes 180256 | tf_op jit(solution)/shard_map/ppermute | solution.py:422
  14.4 9.8 %collective-permute-done.1.refs_2_ = bf16[32,2816]{1,0:T(8,128)(2,1)S(1)} collective-permute-done((bf16[32,2816]{1,0:T(8,128)(2,1)S(1)}, bf16[32,2816]{1,0:T(8,128)(2,1)S(1)}, u32[]{:S(2)}, u32[]{:S(2)}) %collective-permute-start.1) | collective-permute-done | bytes 180256 | tf_op jit(solution)/shard_map/ppermute | solution.py:422
  25.1 8.6 %collective-permute-done.4.near = bf16[32,4608]{1,0:T(8,128)(2,1)S(1)} collective-permute-done((bf16[32,4608]{1,0:T(8,128)(2,1)S(1)}, bf16[32,4608]{1,0:T(8,128)(2,1)S(1)}, u32[]{:S(2)}, u32[]{:S(2)}) %collective-permute-start.4) | collective-permute-done | bytes 294944 | tf_op jit(solution)/shard_map/ppermute | solution.py:422
  43.3 8.0 %collective-permute-done.7.end = bf16[32,4608]{1,0:T(8,128)(2,1)S(1)} collective-permute-done((bf16[32,4608]{1,0:T(8,128)(2,1)S(1)}, bf16[32,4608]{1,0:T(8,128)(2,1)S(1)}, u32[]{:S(2)}, u32[]{:S(2)}) %collective-permute-start.7) | collective-permute-done | bytes 294944 | tf_op jit(solution)/shard_map/ppermute | solution.py:422
  51.3 4.3 %collective-permute-done.8.end_near = bf16[32,4608]{1,0:T(8,128)(2,1)S(1)} collective-permute-done((bf16[32,4608]{1,0:T(8,128)(2,1)S(1)}, bf16[32,4608]{1,0:T(8,128)(2,1)S(1)}, u32[]{:S(2)}, u32[]{:S(2)}) %collective-permute-start.8) | collective-permute-done | bytes 294944 | tf_op jit(solution)/shard_map/ppermute | solution.py:422
  56.6 4.2 %all-to-all-start = ((bf16[32,8,1152]{2,1,0:T(8,128)(2,1)}), bf16[32,8,1152]{2,1,0:T(8,128)(2,1)S(1)}, u32[]{:S(2)}, u32[]{:S(2)}) async-start(bf16[32,8,1152]{2,1,0:T(8,128)(2,1)} %bitcast.6), calls=%async_computation | async-start | bytes 1179648 | tf_op jit(solution)/shard_map/all_to_all | solution.py:549
  60.8 1.9 %shard_map.204 = (bf16[64,3072]{1,0:T(8,128)(2,1)S(1)}, bf16[64,3072]{1,0:T(8,128)(2,1)}, bf16[64,3072]{1,0:T(8,128)(2,1)}, bf16[64,3072]{1,0:T(8,128)(2,1)}) custom-call(bf16[256,256]{1,0:T(8,128)(2,1)S(1)} %shard_map.199.pick_ref, bf16[128,4608]{1,0:T(8,128)(2,1)S(1)} %shard_map.203.own_ref, bf16[128,4608]{1,0:T(8,128)(2,1)S(1)} %collective-permute-done.12.other_ref), custom_call_target="tpu_custom_call" | custom-call | flops 402653184 | bytes 3145728 | tf_op jit(solution)/shard_map/pallas_call | solution.py:466
  63.5 1.8 %collective-permute-start.16 = (bf16[64,3072]{1,0:T(8,128)(2,1)}, bf16[64,3072]{1,0:T(8,128)(2,1)}, u32[]{:S(2)}, u32[]{:S(2)}) collective-permute-start(bf16[64,3072]{1,0:T(8,128)(2,1)} %get-tuple-element.57), channel_id=1, source_target_pairs={{0,8},{4,12},{8,0},{12,4},{16,24},{20,28},{24,16},{28,20},{1,9},{5... | collective-permute-start | bytes 1179656 | tf_op jit(solution)/shard_map/ppermute | solution.py:474
  67.0 9.5 %all-to-all-done = bf16[32,8,1152]{2,1,0:T(8,128)(2,1)S(1)} async-done(((bf16[32,8,1152]{2,1,0:T(8,128)(2,1)}), bf16[32,8,1152]{2,1,0:T(8,128)(2,1)S(1)}, u32[]{:S(2)}, u32[]{:S(2)}) %all-to-all-start) | async-done | bytes 589856 | tf_op jit(solution)/shard_map/all_to_all | solution.py:549
  79.4 4.6 %collective-permute-start.19 = (bf16[64,2560]{1,0:T(8,128)(2,1)S(1)}, bf16[64,2560]{1,0:T(8,128)(2,1)S(1)}, u32[]{:S(2)}, u32[]{:S(2)}) collective-permute-start(bf16[64,2560]{1,0:T(8,128)(2,1)S(1)} %shard_map.207.refs_7_.own_ref), channel_id=1, source_target_pairs={{0,1},{3,2},{4,5},{7,6},{8,9},{11,10},{12,13},{15,14},{16,17},{19,... | collective-permute-start | bytes 983048 | tf_op jit(solution)/shard_map/ppermute | solution.py:422
  84.0 4.5 %shard_map.208 = (f32[256,1024]{1,0:T(8,128)S(1)}, f32[256,64]{1,0:T(8,128)S(1)}) custom-call(bf16[64,2560]{1,0:T(8,128)(2,1)S(1)} %copy-done.18, bf16[64,2560]{1,0:T(8,128)(2,1)S(1)} %copy-done.12, bf16[64,2560]{1,0:T(8,128)(2,1)S(1)} %copy-done.14, bf16[64,2560]{1,0:T(8,128)(2,1)S(1)} %copy-done.16, bf16[1024,7168]{1,0:T(8,128)(2,1)} %bitcast.59, ...), custom_call_target="tpu_custom_call" | custom-call | flops 1342177280 | bytes 6553600 | tf_op jit(solution)/shard_map/pallas_call | solution.py:507
  90.3 3.2 %collective-permute-start.21 = (bf16[64,3072]{1,0:T(8,128)(2,1)S(1)}, bf16[64,3072]{1,0:T(8,128)(2,1)S(1)}, u32[]{:S(2)}, u32[]{:S(2)}) collective-permute-start(bf16[64,3072]{1,0:T(8,128)(2,1)S(1)} %shard_map.209.refs_7_.refs_0_.own_ref), channel_id=1, source_target_pairs={{0,1},{3,2},{4,5},{7,6},{8,9},{11,10},{12,13},{15,14},{16,17},{19,... | collective-permute-start | bytes 1179656 | tf_op jit(solution)/shard_map/ppermute | solution.py:422
  98.3 6.4 %shard_map.210 = (f32[256,1024]{1,0:T(8,128)S(1)}, f32[256,64]{1,0:T(8,128)S(1)}) custom-call(bf16[64,3072]{1,0:T(8,128)(2,1)S(1)} %copy-done.8, bf16[64,3072]{1,0:T(8,128)(2,1)} %collective-permute-done.16.refs_1_, bf16[64,3072]{1,0:T(8,128)(2,1)} %collective-permute-done.17.refs_2_, bf16[64,3072]{1,0:T(8,128)(2,1)} %collective-permute-done.18.refs_3_, ...), custom_call_target="tpu_custom_call" | custom-call | flops 1610612736 | bytes 7864320 | tf_op jit(solution)/shard_map/pallas_call | solution.py:507
  105.9 4.5 %shard_map.213 = (bf16[64,2560]{1,0:T(8,128)(2,1)S(1)}, bf16[256,1152]{1,0:T(8,128)(2,1)}) custom-call(bf16[64,1536]{1,0:T(8,128)(2,1)S(1)} %get-tuple-element.53.refs_5_.refs_0_, bf16[64,1536]{1,0:T(8,128)(2,1)S(1)} %collective-permute-done.13.refs_1_, bf16[64,1536]{1,0:T(8,128)(2,1)S(1)} %collective-permute-done.14.refs_2_, ...), custom_call_target="tpu_custom_call" | custom-call | flops 805306368 | bytes 3932160 | tf_op jit(solution)/shard_map/pallas_call | solution.py:507
  111.2 3.8 %all-to-all-start.1 = ((bf16[32,8,1152]{2,1,0:T(8,128)(2,1)}), bf16[32,8,1152]{2,1,0:T(8,128)(2,1)}, u32[]{:S(2)}, u32[]{:S(2)}) async-start(bf16[32,8,1152]{2,1,0:T(8,128)(2,1)} %bitcast.10), calls=%async_computation.1 | async-start | bytes 1179648 | tf_op jit(solution)/shard_map/all_to_all | solution.py:581
  115.0 3.8 %collective-permute-start.22 = (bf16[64,2560]{1,0:T(8,128)(2,1)S(1)}, bf16[64,2560]{1,0:T(8,128)(2,1)S(1)}, u32[]{:S(2)}, u32[]{:S(2)}) collective-permute-start(bf16[64,2560]{1,0:T(8,128)(2,1)S(1)} %copy-done.10), channel_id=1, source_target_pairs={{0,1},{3,2},{4,5},{7,6},{8,9},{11,10},{12,13},{15,14},{16,17},{19,... | collective-permute-start | bytes 983048 | tf_op jit(solution)/shard_map/ppermute | solution.py:422
  121.4 10.7 %collective-permute-done.22.got_ref.h1 = bf16[64,2560]{1,0:T(8,128)(2,1)S(1)} collective-permute-done((bf16[64,2560]{1,0:T(8,128)(2,1)S(1)}, bf16[64,2560]{1,0:T(8,128)(2,1)S(1)}, u32[]{:S(2)}, u32[]{:S(2)}) %collective-permute-start.22) | collective-permute-done | bytes 327712 | tf_op jit(solution)/shard_map/ppermute | solution.py:422
  135.5 2.5 %shard_map.216 = (bf16[64,7168]{1,0:T(8,128)(2,1)}, bf16[64,7168]{1,0:T(8,128)(2,1)}, bf16[64,7168]{1,0:T(8,128)(2,1)}) custom-call(s32[32]{0:T(128)S(1)} %copy-done.33, bf16[64,2560]{1,0:T(8,128)(2,1)S(1)} %shard_map.207.refs_7_.own_ref, bf16[64,2560]{1,0:T(8,128)(2,1)S(1)} %copy-done.20, bf16[64,2560]{1,0:T(8,128)(2,1)S(1)} %copy-done.22, ...), custom_call_target="tpu_custom_call" | custom-call | flops 3276800 | bytes 3276800 | tf_op jit(solution)/shard_map/pallas_call | solution.py:522
  141.1 10.6 %collective-permute-done.27.h3 = bf16[64,3072]{1,0:T(8,128)(2,1)S(1)} collective-permute-done((bf16[64,3072]{1,0:T(8,128)(2,1)S(1)}, bf16[64,3072]{1,0:T(8,128)(2,1)S(1)}, u32[]{:S(2)}, u32[]{:S(2)}) %collective-permute-start.27) | collective-permute-done | bytes 393248 | tf_op jit(solution)/shard_map/ppermute | solution.py:422
  151.7 2.7 %shard_map.220 = (bf16[64,7168]{1,0:T(8,128)(2,1)}, bf16[64,7168]{1,0:T(8,128)(2,1)}, bf16[64,7168]{1,0:T(8,128)(2,1)}) custom-call(s32[32]{0:T(128)S(1)} %copy-done.33, bf16[64,3072]{1,0:T(8,128)(2,1)S(1)} %shard_map.209.refs_7_.refs_0_.own_ref, bf16[64,3072]{1,0:T(8,128)(2,1)S(1)} %copy-done.5, ...), custom_call_target="tpu_custom_call", output_to_operand_aliasing={{0}: (8, {}), {1}: (9, {}), {2}: (10, {})} | custom-call | flops 3932160 | bytes 3932160 | tf_op jit(solution)/shard_map/pallas_call | solution.py:522
  154.4 3.6 %collective-permute-done.25.h3 = bf16[64,2560]{1,0:T(8,128)(2,1)S(1)} collective-permute-done((bf16[64,2560]{1,0:T(8,128)(2,1)S(1)}, bf16[64,2560]{1,0:T(8,128)(2,1)S(1)}, u32[]{:S(2)}, u32[]{:S(2)}) %collective-permute-start.25) | collective-permute-done | bytes 327712 | tf_op jit(solution)/shard_map/ppermute | solution.py:422
  158.1 2.4 %shard_map.221 = (bf16[64,7168]{1,0:T(8,128)(2,1)}, bf16[64,7168]{1,0:T(8,128)(2,1)}, bf16[64,7168]{1,0:T(8,128)(2,1)}, bf16[64,1024]{1,0:T(8,128)(2,1)}, bf16[6...) custom-call(s32[32]{0:T(128)S(1)} %copy-done.33, ...), custom_call_target="tpu_custom_call", output_to_operand_aliasing={{0}: (11, {}), {1}: (12, {}), {2}: (13, {})} | custom-call | flops 3276800 | bytes 3276800 | tf_op jit(solution)/shard_map/pallas_call | solution.py:522
  160.5 2.3 %shard_map.214 = (bf16[256,1024]{1,0:T(8,128)(2,1)}, bf16[8,32]{1,0:T(8,128)(2,1)}) custom-call(bf16[256,256]{1,0:T(8,128)(2,1)S(1)} %copy-done.28, bf16[256,1152]{1,0:T(8,128)(2,1)} %bitcast.11.ret_ref), custom_call_target="tpu_custom_call" | custom-call | flops 134217728 | bytes 1048576 | tf_op jit(solution)/shard_map/pallas_call | solution.py:587
  (135 shorter events, 37.6 us)
Async XLA Ops:
  3.7 10.6 %collective-permute-start.2 = (bf16[32,2816]{1,0:T(8,128)(2,1)S(1)}, bf16[32,2816]{1,0:T(8,128)(2,1)S(1)}, u32[]{:S(2)}, u32[]{:S(2)}) collective-permute-start(bf16[32,2816]{1,0:T(8,128)(2,1)S(1)} %get-tuple-element.46.refs_0_), channel_id=1, source_target_pairs={{0,3},{1,2},{2,1},{3,0},{4,7},{5,6},{6,5},{7,4},{8,11},{9,10},{10,... | collective-permute-start | bytes 540680 | tf_op jit(solution)/shard_map/ppermute | solution.py:422
  8.9 15.3 %collective-permute-start.1 = (bf16[32,2816]{1,0:T(8,128)(2,1)S(1)}, bf16[32,2816]{1,0:T(8,128)(2,1)S(1)}, u32[]{:S(2)}, u32[]{:S(2)}) collective-permute-start(bf16[32,2816]{1,0:T(8,128)(2,1)S(1)} %get-tuple-element.46.refs_0_), channel_id=1, source_target_pairs={{0,2},{1,3},{2,0},{3,1},{4,6},{5,7},{6,4},{7,5},{8,10},{9,11},{10,... | collective-permute-start | bytes 540680 | tf_op jit(solution)/shard_map/ppermute | solution.py:422
  8.9 15.3 %collective-permute-start = (bf16[32,2816]{1,0:T(8,128)(2,1)S(1)}, bf16[32,2816]{1,0:T(8,128)(2,1)S(1)}, u32[]{:S(2)}, u32[]{:S(2)}) collective-permute-start(bf16[32,2816]{1,0:T(8,128)(2,1)S(1)} %get-tuple-element.46.refs_0_), channel_id=1, source_target_pairs={{0,1},{1,0},{2,3},{3,2},{4,5},{5,4},{6,7},{7,6},{8,9},{9,8},{10,11... | collective-permute-start | bytes 540680 | tf_op jit(solution)/shard_map/ppermute | solution.py:422
  24.2 10.2 %collective-permute-start.3 = (bf16[128,2816]{1,0:T(8,128)(2,1)S(1)}, bf16[128,2816]{1,0:T(8,128)(2,1)S(1)}, u32[]{:S(2)}, u32[]{:S(2)}) collective-permute-start(bf16[128,2816]{1,0:T(8,128)(2,1)S(1)} %shard_map.198.own_ref), channel_id=1, source_target_pairs={{0,4},{4,0},{8,12},{12,8},{16,20},{20,16},{24,28},{28,24},{1,5},{5... | collective-permute-start | bytes 2162696 | tf_op jit(solution)/shard_map/ppermute | solution.py:419
  24.4 14.7 %collective-permute-start.5 = (bf16[32,4608]{1,0:T(8,128)(2,1)S(1)}, bf16[32,4608]{1,0:T(8,128)(2,1)S(1)}, u32[]{:S(2)}, u32[]{:S(2)}) collective-permute-start(bf16[32,4608]{1,0:T(8,128)(2,1)S(1)} %shard_map.200.own), channel_id=1, source_target_pairs={{1,2},{2,1},{5,6},{6,5},{9,10},{10,9},{13,14},{14,13},{17,18},{18,... | collective-permute-start | bytes 884744 | tf_op jit(solution)/shard_map/ppermute | solution.py:422
  35.5 20.1 %collective-permute-start.9 = (bf16[64,2560]{1,0:T(8,128)(2,1)S(1)}, bf16[64,2560]{1,0:T(8,128)(2,1)S(1)}, u32[]{:S(2)}, u32[]{:S(2)}) collective-permute-start(bf16[64,2560]{1,0:T(8,128)(2,1)S(1)} %get-tuple-element.49), channel_id=1, source_target_pairs={{0,8},{4,12},{8,0},{12,4},{16,24},{20,28},{24,16},{28,20},{1,9},{5... | collective-permute-start | bytes 983048 | tf_op jit(solution)/shard_map/ppermute | solution.py:474
  37.1 18.6 %collective-permute-start.10 = (bf16[64,2560]{1,0:T(8,128)(2,1)S(1)}, bf16[64,2560]{1,0:T(8,128)(2,1)S(1)}, u32[]{:S(2)}, u32[]{:S(2)}) collective-permute-start(bf16[64,2560]{1,0:T(8,128)(2,1)S(1)} %get-tuple-element.50), channel_id=1, source_target_pairs={{0,16},{4,20},{8,24},{12,28},{16,0},{20,4},{24,8},{28,12},{1,17},{... | collective-permute-start | bytes 983048 | tf_op jit(solution)/shard_map/ppermute | solution.py:474
  38.6 17.1 %collective-permute-start.11 = (bf16[64,2560]{1,0:T(8,128)(2,1)S(1)}, bf16[64,2560]{1,0:T(8,128)(2,1)S(1)}, u32[]{:S(2)}, u32[]{:S(2)}) collective-permute-start(bf16[64,2560]{1,0:T(8,128)(2,1)S(1)} %get-tuple-element.51), channel_id=1, source_target_pairs={{0,24},{4,28},{8,16},{12,20},{16,8},{20,12},{24,0},{28,4},{1,25},{... | collective-permute-start | bytes 983048 | tf_op jit(solution)/shard_map/ppermute | solution.py:474
  39.1 12.3 %collective-permute-start.7 = (bf16[32,4608]{1,0:T(8,128)(2,1)S(1)}, bf16[32,4608]{1,0:T(8,128)(2,1)S(1)}, u32[]{:S(2)}, u32[]{:S(2)}) collective-permute-start(bf16[32,4608]{1,0:T(8,128)(2,1)S(1)} %collective-permute-done.5.far), channel_id=1, source_target_pairs={{1,0},{2,3},{5,4},{6,7},{9,8},{10,11},{13,12},{14,15},{17,16},{18,... | collective-permute-start | bytes 884744 | tf_op jit(solution)/shard_map/ppermute | solution.py:422
  40.4 15.3 %collective-permute-start.8 = (bf16[32,4608]{1,0:T(8,128)(2,1)S(1)}, bf16[32,4608]{1,0:T(8,128)(2,1)S(1)}, u32[]{:S(2)}, u32[]{:S(2)}) collective-permute-start(bf16[32,4608]{1,0:T(8,128)(2,1)S(1)} %collective-permute-done.6.far_near), channel_id=1, source_target_pairs={{1,0},{2,3},{5,4},{6,7},{9,8},{10,11},{13,12},{14,15},{17,16},{18,... | collective-permute-start | bytes 884744 | tf_op jit(solution)/shard_map/ppermute | solution.py:422
  56.6 19.9 %all-to-all-start = ((bf16[32,8,1152]{2,1,0:T(8,128)(2,1)}), bf16[32,8,1152]{2,1,0:T(8,128)(2,1)S(1)}, u32[]{:S(2)}, u32[]{:S(2)}) async-start(bf16[32,8,1152]{2,1,0:T(8,128)(2,1)} %bitcast.6), calls=%async_computation | async-start | bytes 1179648 | tf_op jit(solution)/shard_map/all_to_all | solution.py:549
  63.5 25.0 %collective-permute-start.16 = (bf16[64,3072]{1,0:T(8,128)(2,1)}, bf16[64,3072]{1,0:T(8,128)(2,1)}, u32[]{:S(2)}, u32[]{:S(2)}) collective-permute-start(bf16[64,3072]{1,0:T(8,128)(2,1)} %get-tuple-element.57), channel_id=1, source_target_pairs={{0,8},{4,12},{8,0},{12,4},{16,24},{20,28},{24,16},{28,20},{1,9},{5... | collective-permute-start | bytes 1179656 | tf_op jit(solution)/shard_map/ppermute | solution.py:474
  65.3 23.3 %collective-permute-start.17 = (bf16[64,3072]{1,0:T(8,128)(2,1)}, bf16[64,3072]{1,0:T(8,128)(2,1)}, u32[]{:S(2)}, u32[]{:S(2)}) collective-permute-start(bf16[64,3072]{1,0:T(8,128)(2,1)} %get-tuple-element.58), channel_id=1, source_target_pairs={{0,16},{4,20},{8,24},{12,28},{16,0},{20,4},{24,8},{28,12},{1,17},{... | collective-permute-start | bytes 1179656 | tf_op jit(solution)/shard_map/ppermute | solution.py:474
  66.8 21.8 %collective-permute-start.18 = (bf16[64,3072]{1,0:T(8,128)(2,1)}, bf16[64,3072]{1,0:T(8,128)(2,1)}, u32[]{:S(2)}, u32[]{:S(2)}) collective-permute-start(bf16[64,3072]{1,0:T(8,128)(2,1)} %get-tuple-element.59), channel_id=1, source_target_pairs={{0,24},{4,28},{8,16},{12,20},{16,8},{20,12},{24,0},{28,4},{1,25},{... | collective-permute-start | bytes 1179656 | tf_op jit(solution)/shard_map/ppermute | solution.py:474
  79.4 14.1 %collective-permute-start.19 = (bf16[64,2560]{1,0:T(8,128)(2,1)S(1)}, bf16[64,2560]{1,0:T(8,128)(2,1)S(1)}, u32[]{:S(2)}, u32[]{:S(2)}) collective-permute-start(bf16[64,2560]{1,0:T(8,128)(2,1)S(1)} %shard_map.207.refs_7_.own_ref), channel_id=1, source_target_pairs={{0,1},{3,2},{4,5},{7,6},{8,9},{11,10},{12,13},{15,14},{16,17},{19,... | collective-permute-start | bytes 983048 | tf_op jit(solution)/shard_map/ppermute | solution.py:422
  90.3 15.6 %collective-permute-start.21 = (bf16[64,3072]{1,0:T(8,128)(2,1)S(1)}, bf16[64,3072]{1,0:T(8,128)(2,1)S(1)}, u32[]{:S(2)}, u32[]{:S(2)}) collective-permute-start(bf16[64,3072]{1,0:T(8,128)(2,1)S(1)} %shard_map.209.refs_7_.refs_0_.own_ref), channel_id=1, source_target_pairs={{0,1},{3,2},{4,5},{7,6},{8,9},{11,10},{12,13},{15,14},{16,17},{19,... | collective-permute-start | bytes 1179656 | tf_op jit(solution)/shard_map/ppermute | solution.py:422
  94.1 10.7 %collective-permute-start.20 = (bf16[64,2560]{1,0:T(8,128)(2,1)S(1)}, bf16[64,2560]{1,0:T(8,128)(2,1)S(1)}, u32[]{:S(2)}, u32[]{:S(2)}) collective-permute-start(bf16[64,2560]{1,0:T(8,128)(2,1)S(1)} %shard_map.211), channel_id=1, source_target_pairs={{1,2},{2,1},{5,6},{6,5},{9,10},{10,9},{13,14},{14,13},{17,18},{18,... | collective-permute-start | bytes 983048 | tf_op jit(solution)/shard_map/ppermute | solution.py:422
  94.8 10.8 %collective-permute-start.13 = (bf16[64,1536]{1,0:T(8,128)(2,1)S(1)}, bf16[64,1536]{1,0:T(8,128)(2,1)S(1)}, u32[]{:S(2)}, u32[]{:S(2)}) collective-permute-start(bf16[64,1536]{1,0:T(8,128)(2,1)S(1)} %get-tuple-element.54), channel_id=1, source_target_pairs={{0,8},{4,12},{8,0},{12,4},{16,24},{20,28},{24,16},{28,20},{1,9},{5... | collective-permute-start | bytes 589832 | tf_op jit(solution)/shard_map/ppermute | solution.py:474
  111.2 49.3 %all-to-all-start.1 = ((bf16[32,8,1152]{2,1,0:T(8,128)(2,1)}), bf16[32,8,1152]{2,1,0:T(8,128)(2,1)}, u32[]{:S(2)}, u32[]{:S(2)}) async-start(bf16[32,8,1152]{2,1,0:T(8,128)(2,1)} %bitcast.10), calls=%async_computation.1 | async-start | bytes 1179648 | tf_op jit(solution)/shard_map/all_to_all | solution.py:581
  115.0 17.1 %collective-permute-start.22 = (bf16[64,2560]{1,0:T(8,128)(2,1)S(1)}, bf16[64,2560]{1,0:T(8,128)(2,1)S(1)}, u32[]{:S(2)}, u32[]{:S(2)}) collective-permute-start(bf16[64,2560]{1,0:T(8,128)(2,1)S(1)} %copy-done.10), channel_id=1, source_target_pairs={{0,1},{3,2},{4,5},{7,6},{8,9},{11,10},{12,13},{15,14},{16,17},{19,... | collective-permute-start | bytes 983048 | tf_op jit(solution)/shard_map/ppermute | solution.py:422
  119.4 14.2 %collective-permute-start.26 = (bf16[64,3072]{1,0:T(8,128)(2,1)S(1)}, bf16[64,3072]{1,0:T(8,128)(2,1)S(1)}, u32[]{:S(2)}, u32[]{:S(2)}) collective-permute-start(bf16[64,3072]{1,0:T(8,128)(2,1)S(1)} %shard_map.218), channel_id=1, source_target_pairs={{1,2},{2,1},{5,6},{6,5},{9,10},{10,9},{13,14},{14,13},{17,18},{18,... | collective-permute-start | bytes 1179656 | tf_op jit(solution)/shard_map/ppermute | solution.py:422
  120.1 15.4 %collective-permute-start.24 = (bf16[64,2560]{1,0:T(8,128)(2,1)S(1)}, bf16[64,2560]{1,0:T(8,128)(2,1)S(1)}, u32[]{:S(2)}, u32[]{:S(2)}) collective-permute-start(bf16[64,2560]{1,0:T(8,128)(2,1)S(1)} %copy-done.24), channel_id=1, source_target_pairs={{1,0},{2,3},{5,4},{6,7},{9,8},{10,11},{13,12},{14,15},{17,16},{18,... | collective-permute-start | bytes 983048 | tf_op jit(solution)/shard_map/ppermute | solution.py:422
  134.1 17.5 %collective-permute-start.27 = (bf16[64,3072]{1,0:T(8,128)(2,1)S(1)}, bf16[64,3072]{1,0:T(8,128)(2,1)S(1)}, u32[]{:S(2)}, u32[]{:S(2)}) collective-permute-start(bf16[64,3072]{1,0:T(8,128)(2,1)S(1)} %shard_map.219), channel_id=1, source_target_pairs={{1,0},{2,3},{5,4},{6,7},{9,8},{10,11},{13,12},{14,15},{17,16},{18,... | collective-permute-start | bytes 1179656 | tf_op jit(solution)/shard_map/ppermute | solution.py:422
  139.8 18.3 %collective-permute-start.25 = (bf16[64,2560]{1,0:T(8,128)(2,1)S(1)}, bf16[64,2560]{1,0:T(8,128)(2,1)S(1)}, u32[]{:S(2)}, u32[]{:S(2)}) collective-permute-start(bf16[64,2560]{1,0:T(8,128)(2,1)S(1)} %shard_map.217), channel_id=1, source_target_pairs={{1,0},{2,3},{5,4},{6,7},{9,8},{10,11},{13,12},{14,15},{17,16},{18,... | collective-permute-start | bytes 983048 | tf_op jit(solution)/shard_map/ppermute | solution.py:422
  (43 other events, 236.1 us)

commit v4 on v3

--- a/solution.py
+++ b/solution.py
@@ -423,7 +423,7 @@
 
     got = [send(chunk0, [(i, i ^ s) for i in range(members)]) for s in range(1, members)]
 
-    rest = tied(rest, *got)
+    rest = tied(rest, got[0])
     middle, outer = [(1, 2), (2, 1)], [(1, 0), (2, 3)]
     near = send(rest, [(0, 1), (1, 0), (2, 3), (3, 2)])
     far = send(rest, middle)

time: 164 us -> 164 us (level)
  no operation moved by 1% of the time
where the time goes in v4:
time: 164 us; the launch traced here: 163 us
  waiting for transfers between devices  70.3 us (43%)
  starting transfers between devices  46 us (28%)
  Pallas kernels  37.5 us (23%)
  local copies, waits for them, and re-layouts  7.6 us (5%)
    ppermute x17, waiting for transfers between devices, send(): return lax.ppermute(x, 'ex', pairs)  60.6 us
    ppermute x17, starting transfers between devices, send(): return lax.ppermute(x, 'ex', pairs)  27.3 us
    pallas_call x3, Pallas kernels, expert(): call(functools.partial(expert_kernel, steps, off, len(after), not carry,...  15.5 us
    ppermute x9, starting transfers between devices, plane_rows(): lax.ppermute(blocks[s], 'ep', [(i, i ^ 2 * s) for i in range(groups)])  10.6 us
    all_to_all x1, waiting for transfers between devices, per_device(): lax.all_to_all(outgoing.reshape(slots, cap, hidden + LANES), ('ep', 'ex')...  9.46 us
    pallas_call x3, Pallas kernels, adam(): call(functools.partial(adam_kernel, members, parts, carried + len(after))...  7.61 us
    unnamed x74, local copies, waits for them, and re-layouts  7.6 us
    all_to_all x1, starting transfers between devices, per_device(): lax.all_to_all(outgoing.reshape(slots, cap, hidden + LANES), ('ep', 'ex')...  4.2 us
  transfers between devices with their start and end apart: 30, of which 10 were waited for; matrix products, arithmetic and copies ran while one was open for 0% of the time, Pallas kernels for 18%

profile of v4, /device:TPU:0, one launch (start us, length us, event | category | flops | bytes accessed | tf_op | source)
XLA Modules:
  0.0 162.8 jit_solution(17494181384629225026)
XLA Ops:
  3.7 5.1 %collective-permute-start.2 = (bf16[32,2816]{1,0:T(8,128)(2,1)S(1)}, bf16[32,2816]{1,0:T(8,128)(2,1)S(1)}, u32[]{:S(2)}, u32[]{:S(2)}) collective-permute-start(bf16[32,2816]{1,0:T(8,128)(2,1)S(1)} %get-tuple-element.46.refs_0_), channel_id=1, source_target_pairs={{0,3},{1,2},{2,1},{3,0},{4,7},{5,6},{6,5},{7,4},{8,11},{9,10},{10,... | collective-permute-start | bytes 540680 | tf_op jit(solution)/shard_map/ppermute | solution.py:422
  9.5 4.9 %collective-permute-done.2.refs_3_ = bf16[32,2816]{1,0:T(8,128)(2,1)S(1)} collective-permute-done((bf16[32,2816]{1,0:T(8,128)(2,1)S(1)}, bf16[32,2816]{1,0:T(8,128)(2,1)S(1)}, u32[]{:S(2)}, u32[]{:S(2)}) %collective-permute-start.2) | collective-permute-done | bytes 180256 | tf_op jit(solution)/shard_map/ppermute | solution.py:422
  14.4 9.8 %collective-permute-done.1.refs_2_ = bf16[32,2816]{1,0:T(8,128)(2,1)S(1)} collective-permute-done((bf16[32,2816]{1,0:T(8,128)(2,1)S(1)}, bf16[32,2816]{1,0:T(8,128)(2,1)S(1)}, u32[]{:S(2)}, u32[]{:S(2)}) %collective-permute-start.1) | collective-permute-done | bytes 180256 | tf_op jit(solution)/shard_map/ppermute | solution.py:422
  25.1 8.6 %collective-permute-done.4.near = bf16[32,4608]{1,0:T(8,128)(2,1)S(1)} collective-permute-done((bf16[32,4608]{1,0:T(8,128)(2,1)S(1)}, bf16[32,4608]{1,0:T(8,128)(2,1)S(1)}, u32[]{:S(2)}, u32[]{:S(2)}) %collective-permute-start.4) | collective-permute-done | bytes 294944 | tf_op jit(solution)/shard_map/ppermute | solution.py:422
  43.3 8.0 %collective-permute-done.7.end = bf16[32,4608]{1,0:T(8,128)(2,1)S(1)} collective-permute-done((bf16[32,4608]{1,0:T(8,128)(2,1)S(1)}, bf16[32,4608]{1,0:T(8,128)(2,1)S(1)}, u32[]{:S(2)}, u32[]{:S(2)}) %collective-permute-start.7) | collective-permute-done | bytes 294944 | tf_op jit(solution)/shard_map/ppermute | solution.py:422
  51.3 4.3 %collective-permute-done.8.end_near = bf16[32,4608]{1,0:T(8,128)(2,1)S(1)} collective-permute-done((bf16[32,4608]{1,0:T(8,128)(2,1)S(1)}, bf16[32,4608]{1,0:T(8,128)(2,1)S(1)}, u32[]{:S(2)}, u32[]{:S(2)}) %collective-permute-start.8) | collective-permute-done | bytes 294944 | tf_op jit(solution)/shard_map/ppermute | solution.py:422
  56.6 4.2 %all-to-all-start = ((bf16[32,8,1152]{2,1,0:T(8,128)(2,1)}), bf16[32,8,1152]{2,1,0:T(8,128)(2,1)S(1)}, u32[]{:S(2)}, u32[]{:S(2)}) async-start(bf16[32,8,1152]{2,1,0:T(8,128)(2,1)} %bitcast.6), calls=%async_computation | async-start | bytes 1179648 | tf_op jit(solution)/shard_map/all_to_all | solution.py:549
  60.8 1.9 %shard_map.204 = (bf16[64,3072]{1,0:T(8,128)(2,1)S(1)}, bf16[64,3072]{1,0:T(8,128)(2,1)}, bf16[64,3072]{1,0:T(8,128)(2,1)}, bf16[64,3072]{1,0:T(8,128)(2,1)}) custom-call(bf16[256,256]{1,0:T(8,128)(2,1)S(1)} %shard_map.199.pick_ref, bf16[128,4608]{1,0:T(8,128)(2,1)S(1)} %shard_map.203.own_ref, bf16[128,4608]{1,0:T(8,128)(2,1)S(1)} %collective-permute-done.12.other_ref), custom_call_target="tpu_custom_call" | custom-call | flops 402653184 | bytes 3145728 | tf_op jit(solution)/shard_map/pallas_call | solution.py:466
  63.5 1.8 %collective-permute-start.16 = (bf16[64,3072]{1,0:T(8,128)(2,1)}, bf16[64,3072]{1,0:T(8,128)(2,1)}, u32[]{:S(2)}, u32[]{:S(2)}) collective-permute-start(bf16[64,3072]{1,0:T(8,128)(2,1)} %get-tuple-element.57), channel_id=1, source_target_pairs={{0,8},{4,12},{8,0},{12,4},{16,24},{20,28},{24,16},{28,20},{1,9},{5... | collective-permute-start | bytes 1179656 | tf_op jit(solution)/shard_map/ppermute | solution.py:474
  67.0 9.5 %all-to-all-done = bf16[32,8,1152]{2,1,0:T(8,128)(2,1)S(1)} async-done(((bf16[32,8,1152]{2,1,0:T(8,128)(2,1)}), bf16[32,8,1152]{2,1,0:T(8,128)(2,1)S(1)}, u32[]{:S(2)}, u32[]{:S(2)}) %all-to-all-start) | async-done | bytes 589856 | tf_op jit(solution)/shard_map/all_to_all | solution.py:549
  79.4 4.6 %collective-permute-start.19 = (bf16[64,2560]{1,0:T(8,128)(2,1)S(1)}, bf16[64,2560]{1,0:T(8,128)(2,1)S(1)}, u32[]{:S(2)}, u32[]{:S(2)}) collective-permute-start(bf16[64,2560]{1,0:T(8,128)(2,1)S(1)} %shard_map.207.refs_7_.own_ref), channel_id=1, source_target_pairs={{0,1},{3,2},{4,5},{7,6},{8,9},{11,10},{12,13},{15,14},{16,17},{19,... | collective-permute-start | bytes 983048 | tf_op jit(solution)/shard_map/ppermute | solution.py:422
  84.0 4.5 %shard_map.208 = (f32[256,1024]{1,0:T(8,128)S(1)}, f32[256,64]{1,0:T(8,128)S(1)}) custom-call(bf16[64,2560]{1,0:T(8,128)(2,1)S(1)} %copy-done.18, bf16[64,2560]{1,0:T(8,128)(2,1)S(1)} %copy-done.12, bf16[64,2560]{1,0:T(8,128)(2,1)S(1)} %copy-done.14, bf16[64,2560]{1,0:T(8,128)(2,1)S(1)} %copy-done.16, bf16[1024,7168]{1,0:T(8,128)(2,1)} %bitcast.59, ...), custom_call_target="tpu_custom_call" | custom-call | flops 1342177280 | bytes 6553600 | tf_op jit(solution)/shard_map/pallas_call | solution.py:507
  90.3 3.2 %collective-permute-start.21 = (bf16[64,3072]{1,0:T(8,128)(2,1)S(1)}, bf16[64,3072]{1,0:T(8,128)(2,1)S(1)}, u32[]{:S(2)}, u32[]{:S(2)}) collective-permute-start(bf16[64,3072]{1,0:T(8,128)(2,1)S(1)} %shard_map.209.refs_7_.refs_0_.own_ref), channel_id=1, source_target_pairs={{0,1},{3,2},{4,5},{7,6},{8,9},{11,10},{12,13},{15,14},{16,17},{19,... | collective-permute-start | bytes 1179656 | tf_op jit(solution)/shard_map/ppermute | solution.py:422
  98.3 6.4 %shard_map.210 = (f32[256,1024]{1,0:T(8,128)S(1)}, f32[256,64]{1,0:T(8,128)S(1)}) custom-call(bf16[64,3072]{1,0:T(8,128)(2,1)S(1)} %copy-done.8, bf16[64,3072]{1,0:T(8,128)(2,1)} %collective-permute-done.16.refs_1_, bf16[64,3072]{1,0:T(8,128)(2,1)} %collective-permute-done.17.refs_2_, bf16[64,3072]{1,0:T(8,128)(2,1)} %collective-permute-done.18.refs_3_, ...), custom_call_target="tpu_custom_call" | custom-call | flops 1610612736 | bytes 7864320 | tf_op jit(solution)/shard_map/pallas_call | solution.py:507
  105.9 4.5 %shard_map.213 = (bf16[64,2560]{1,0:T(8,128)(2,1)S(1)}, bf16[256,1152]{1,0:T(8,128)(2,1)}) custom-call(bf16[64,1536]{1,0:T(8,128)(2,1)S(1)} %get-tuple-element.53.refs_5_.refs_0_, bf16[64,1536]{1,0:T(8,128)(2,1)S(1)} %collective-permute-done.13.refs_1_, bf16[64,1536]{1,0:T(8,128)(2,1)S(1)} %collective-permute-done.14.refs_2_, ...), custom_call_target="tpu_custom_call" | custom-call | flops 805306368 | bytes 3932160 | tf_op jit(solution)/shard_map/pallas_call | solution.py:507
  111.2 3.8 %all-to-all-start.1 = ((bf16[32,8,1152]{2,1,0:T(8,128)(2,1)}), bf16[32,8,1152]{2,1,0:T(8,128)(2,1)}, u32[]{:S(2)}, u32[]{:S(2)}) async-start(bf16[32,8,1152]{2,1,0:T(8,128)(2,1)} %bitcast.10), calls=%async_computation.1 | async-start | bytes 1179648 | tf_op jit(solution)/shard_map/all_to_all | solution.py:581
  115.0 3.8 %collective-permute-start.22 = (bf16[64,2560]{1,0:T(8,128)(2,1)S(1)}, bf16[64,2560]{1,0:T(8,128)(2,1)S(1)}, u32[]{:S(2)}, u32[]{:S(2)}) collective-permute-start(bf16[64,2560]{1,0:T(8,128)(2,1)S(1)} %copy-done.10), channel_id=1, source_target_pairs={{0,1},{3,2},{4,5},{7,6},{8,9},{11,10},{12,13},{15,14},{16,17},{19,... | collective-permute-start | bytes 983048 | tf_op jit(solution)/shard_map/ppermute | solution.py:422
  121.4 10.7 %collective-permute-done.22.got_ref.h1 = bf16[64,2560]{1,0:T(8,128)(2,1)S(1)} collective-permute-done((bf16[64,2560]{1,0:T(8,128)(2,1)S(1)}, bf16[64,2560]{1,0:T(8,128)(2,1)S(1)}, u32[]{:S(2)}, u32[]{:S(2)}) %collective-permute-start.22) | collective-permute-done | bytes 327712 | tf_op jit(solution)/shard_map/ppermute | solution.py:422
  135.5 2.5 %shard_map.216 = (bf16[64,7168]{1,0:T(8,128)(2,1)}, bf16[64,7168]{1,0:T(8,128)(2,1)}, bf16[64,7168]{1,0:T(8,128)(2,1)}) custom-call(s32[32]{0:T(128)S(1)} %copy-done.33, bf16[64,2560]{1,0:T(8,128)(2,1)S(1)} %shard_map.207.refs_7_.own_ref, bf16[64,2560]{1,0:T(8,128)(2,1)S(1)} %copy-done.20, bf16[64,2560]{1,0:T(8,128)(2,1)S(1)} %copy-done.22, ...), custom_call_target="tpu_custom_call" | custom-call | flops 3276800 | bytes 3276800 | tf_op jit(solution)/shard_map/pallas_call | solution.py:522
  141.1 10.6 %collective-permute-done.27.h3 = bf16[64,3072]{1,0:T(8,128)(2,1)S(1)} collective-permute-done((bf16[64,3072]{1,0:T(8,128)(2,1)S(1)}, bf16[64,3072]{1,0:T(8,128)(2,1)S(1)}, u32[]{:S(2)}, u32[]{:S(2)}) %collective-permute-start.27) | collective-permute-done | bytes 393248 | tf_op jit(solution)/shard_map/ppermute | solution.py:422
  151.7 2.7 %shard_map.220 = (bf16[64,7168]{1,0:T(8,128)(2,1)}, bf16[64,7168]{1,0:T(8,128)(2,1)}, bf16[64,7168]{1,0:T(8,128)(2,1)}) custom-call(s32[32]{0:T(128)S(1)} %copy-done.33, bf16[64,3072]{1,0:T(8,128)(2,1)S(1)} %shard_map.209.refs_7_.refs_0_.own_ref, bf16[64,3072]{1,0:T(8,128)(2,1)S(1)} %copy-done.5, ...), custom_call_target="tpu_custom_call", output_to_operand_aliasing={{0}: (8, {}), {1}: (9, {}), {2}: (10, {})} | custom-call | flops 3932160 | bytes 3932160 | tf_op jit(solution)/shard_map/pallas_call | solution.py:522
  154.4 3.6 %collective-permute-done.25.h3 = bf16[64,2560]{1,0:T(8,128)(2,1)S(1)} collective-permute-done((bf16[64,2560]{1,0:T(8,128)(2,1)S(1)}, bf16[64,2560]{1,0:T(8,128)(2,1)S(1)}, u32[]{:S(2)}, u32[]{:S(2)}) %collective-permute-start.25) | collective-permute-done | bytes 327712 | tf_op jit(solution)/shard_map/ppermute | solution.py:422
  158.1 2.4 %shard_map.221 = (bf16[64,7168]{1,0:T(8,128)(2,1)}, bf16[64,7168]{1,0:T(8,128)(2,1)}, bf16[64,7168]{1,0:T(8,128)(2,1)}, bf16[64,1024]{1,0:T(8,128)(2,1)}, bf16[6...) custom-call(s32[32]{0:T(128)S(1)} %copy-done.33, ...), custom_call_target="tpu_custom_call", output_to_operand_aliasing={{0}: (11, {}), {1}: (12, {}), {2}: (13, {})} | custom-call | flops 3276800 | bytes 3276800 | tf_op jit(solution)/shard_map/pallas_call | solution.py:522
  160.5 2.3 %shard_map.214 = (bf16[256,1024]{1,0:T(8,128)(2,1)}, bf16[8,32]{1,0:T(8,128)(2,1)}) custom-call(bf16[256,256]{1,0:T(8,128)(2,1)S(1)} %copy-done.28, bf16[256,1152]{1,0:T(8,128)(2,1)} %bitcast.11.ret_ref), custom_call_target="tpu_custom_call" | custom-call | flops 134217728 | bytes 1048576 | tf_op jit(solution)/shard_map/pallas_call | solution.py:587
  (135 shorter events, 37.6 us)
Async XLA Ops:
  3.7 10.6 %collective-permute-start.2 = (bf16[32,2816]{1,0:T(8,128)(2,1)S(1)}, bf16[32,2816]{1,0:T(8,128)(2,1)S(1)}, u32[]{:S(2)}, u32[]{:S(2)}) collective-permute-start(bf16[32,2816]{1,0:T(8,128)(2,1)S(1)} %get-tuple-element.46.refs_0_), channel_id=1, source_target_pairs={{0,3},{1,2},{2,1},{3,0},{4,7},{5,6},{6,5},{7,4},{8,11},{9,10},{10,... | collective-permute-start | bytes 540680 | tf_op jit(solution)/shard_map/ppermute | solution.py:422
  8.9 15.3 %collective-permute-start.1 = (bf16[32,2816]{1,0:T(8,128)(2,1)S(1)}, bf16[32,2816]{1,0:T(8,128)(2,1)S(1)}, u32[]{:S(2)}, u32[]{:S(2)}) collective-permute-start(bf16[32,2816]{1,0:T(8,128)(2,1)S(1)} %get-tuple-element.46.refs_0_), channel_id=1, source_target_pairs={{0,2},{1,3},{2,0},{3,1},{4,6},{5,7},{6,4},{7,5},{8,10},{9,11},{10,... | collective-permute-start | bytes 540680 | tf_op jit(solution)/shard_map/ppermute | solution.py:422
  8.9 15.3 %collective-permute-start = (bf16[32,2816]{1,0:T(8,128)(2,1)S(1)}, bf16[32,2816]{1,0:T(8,128)(2,1)S(1)}, u32[]{:S(2)}, u32[]{:S(2)}) collective-permute-start(bf16[32,2816]{1,0:T(8,128)(2,1)S(1)} %get-tuple-element.46.refs_0_), channel_id=1, source_target_pairs={{0,1},{1,0},{2,3},{3,2},{4,5},{5,4},{6,7},{7,6},{8,9},{9,8},{10,11... | collective-permute-start | bytes 540680 | tf_op jit(solution)/shard_map/ppermute | solution.py:422
  24.2 10.2 %collective-permute-start.3 = (bf16[128,2816]{1,0:T(8,128)(2,1)S(1)}, bf16[128,2816]{1,0:T(8,128)(2,1)S(1)}, u32[]{:S(2)}, u32[]{:S(2)}) collective-permute-start(bf16[128,2816]{1,0:T(8,128)(2,1)S(1)} %shard_map.198.own_ref), channel_id=1, source_target_pairs={{0,4},{4,0},{8,12},{12,8},{16,20},{20,16},{24,28},{28,24},{1,5},{5... | collective-permute-start | bytes 2162696 | tf_op jit(solution)/shard_map/ppermute | solution.py:419
  24.4 14.7 %collective-permute-start.5 = (bf16[32,4608]{1,0:T(8,128)(2,1)S(1)}, bf16[32,4608]{1,0:T(8,128)(2,1)S(1)}, u32[]{:S(2)}, u32[]{:S(2)}) collective-permute-start(bf16[32,4608]{1,0:T(8,128)(2,1)S(1)} %shard_map.200.own), channel_id=1, source_target_pairs={{1,2},{2,1},{5,6},{6,5},{9,10},{10,9},{13,14},{14,13},{17,18},{18,... | collective-permute-start | bytes 884744 | tf_op jit(solution)/shard_map/ppermute | solution.py:422
  35.5 20.1 %collective-permute-start.9 = (bf16[64,2560]{1,0:T(8,128)(2,1)S(1)}, bf16[64,2560]{1,0:T(8,128)(2,1)S(1)}, u32[]{:S(2)}, u32[]{:S(2)}) collective-permute-start(bf16[64,2560]{1,0:T(8,128)(2,1)S(1)} %get-tuple-element.49), channel_id=1, source_target_pairs={{0,8},{4,12},{8,0},{12,4},{16,24},{20,28},{24,16},{28,20},{1,9},{5... | collective-permute-start | bytes 983048 | tf_op jit(solution)/shard_map/ppermute | solution.py:474
  37.1 18.6 %collective-permute-start.10 = (bf16[64,2560]{1,0:T(8,128)(2,1)S(1)}, bf16[64,2560]{1,0:T(8,128)(2,1)S(1)}, u32[]{:S(2)}, u32[]{:S(2)}) collective-permute-start(bf16[64,2560]{1,0:T(8,128)(2,1)S(1)} %get-tuple-element.50), channel_id=1, source_target_pairs={{0,16},{4,20},{8,24},{12,28},{16,0},{20,4},{24,8},{28,12},{1,17},{... | collective-permute-start | bytes 983048 | tf_op jit(solution)/shard_map/ppermute | solution.py:474
  38.6 17.1 %collective-permute-start.11 = (bf16[64,2560]{1,0:T(8,128)(2,1)S(1)}, bf16[64,2560]{1,0:T(8,128)(2,1)S(1)}, u32[]{:S(2)}, u32[]{:S(2)}) collective-permute-start(bf16[64,2560]{1,0:T(8,128)(2,1)S(1)} %get-tuple-element.51), channel_id=1, source_target_pairs={{0,24},{4,28},{8,16},{12,20},{16,8},{20,12},{24,0},{28,4},{1,25},{... | collective-permute-start | bytes 983048 | tf_op jit(solution)/shard_map/ppermute | solution.py:474
  39.1 12.3 %collective-permute-start.7 = (bf16[32,4608]{1,0:T(8,128)(2,1)S(1)}, bf16[32,4608]{1,0:T(8,128)(2,1)S(1)}, u32[]{:S(2)}, u32[]{:S(2)}) collective-permute-start(bf16[32,4608]{1,0:T(8,128)(2,1)S(1)} %collective-permute-done.5.far), channel_id=1, source_target_pairs={{1,0},{2,3},{5,4},{6,7},{9,8},{10,11},{13,12},{14,15},{17,16},{18,... | collective-permute-start | bytes 884744 | tf_op jit(solution)/shard_map/ppermute | solution.py:422
  40.4 15.3 %collective-permute-start.8 = (bf16[32,4608]{1,0:T(8,128)(2,1)S(1)}, bf16[32,4608]{1,0:T(8,128)(2,1)S(1)}, u32[]{:S(2)}, u32[]{:S(2)}) collective-permute-start(bf16[32,4608]{1,0:T(8,128)(2,1)S(1)} %collective-permute-done.6.far_near), channel_id=1, source_target_pairs={{1,0},{2,3},{5,4},{6,7},{9,8},{10,11},{13,12},{14,15},{17,16},{18,... | collective-permute-start | bytes 884744 | tf_op jit(solution)/shard_map/ppermute | solution.py:422
  56.6 19.9 %all-to-all-start = ((bf16[32,8,1152]{2,1,0:T(8,128)(2,1)}), bf16[32,8,1152]{2,1,0:T(8,128)(2,1)S(1)}, u32[]{:S(2)}, u32[]{:S(2)}) async-start(bf16[32,8,1152]{2,1,0:T(8,128)(2,1)} %bitcast.6), calls=%async_computation | async-start | bytes 1179648 | tf_op jit(solution)/shard_map/all_to_all | solution.py:549
  63.5 25.0 %collective-permute-start.16 = (bf16[64,3072]{1,0:T(8,128)(2,1)}, bf16[64,3072]{1,0:T(8,128)(2,1)}, u32[]{:S(2)}, u32[]{:S(2)}) collective-permute-start(bf16[64,3072]{1,0:T(8,128)(2,1)} %get-tuple-element.57), channel_id=1, source_target_pairs={{0,8},{4,12},{8,0},{12,4},{16,24},{20,28},{24,16},{28,20},{1,9},{5... | collective-permute-start | bytes 1179656 | tf_op jit(solution)/shard_map/ppermute | solution.py:474
  65.3 23.3 %collective-permute-start.17 = (bf16[64,3072]{1,0:T(8,128)(2,1)}, bf16[64,3072]{1,0:T(8,128)(2,1)}, u32[]{:S(2)}, u32[]{:S(2)}) collective-permute-start(bf16[64,3072]{1,0:T(8,128)(2,1)} %get-tuple-element.58), channel_id=1, source_target_pairs={{0,16},{4,20},{8,24},{12,28},{16,0},{20,4},{24,8},{28,12},{1,17},{... | collective-permute-start | bytes 1179656 | tf_op jit(solution)/shard_map/ppermute | solution.py:474
  66.8 21.8 %collective-permute-start.18 = (bf16[64,3072]{1,0:T(8,128)(2,1)}, bf16[64,3072]{1,0:T(8,128)(2,1)}, u32[]{:S(2)}, u32[]{:S(2)}) collective-permute-start(bf16[64,3072]{1,0:T(8,128)(2,1)} %get-tuple-element.59), channel_id=1, source_target_pairs={{0,24},{4,28},{8,16},{12,20},{16,8},{20,12},{24,0},{28,4},{1,25},{... | collective-permute-start | bytes 1179656 | tf_op jit(solution)/shard_map/ppermute | solution.py:474
  79.4 14.1 %collective-permute-start.19 = (bf16[64,2560]{1,0:T(8,128)(2,1)S(1)}, bf16[64,2560]{1,0:T(8,128)(2,1)S(1)}, u32[]{:S(2)}, u32[]{:S(2)}) collective-permute-start(bf16[64,2560]{1,0:T(8,128)(2,1)S(1)} %shard_map.207.refs_7_.own_ref), channel_id=1, source_target_pairs={{0,1},{3,2},{4,5},{7,6},{8,9},{11,10},{12,13},{15,14},{16,17},{19,... | collective-permute-start | bytes 983048 | tf_op jit(solution)/shard_map/ppermute | solution.py:422
  90.3 15.6 %collective-permute-start.21 = (bf16[64,3072]{1,0:T(8,128)(2,1)S(1)}, bf16[64,3072]{1,0:T(8,128)(2,1)S(1)}, u32[]{:S(2)}, u32[]{:S(2)}) collective-permute-start(bf16[64,3072]{1,0:T(8,128)(2,1)S(1)} %shard_map.209.refs_7_.refs_0_.own_ref), channel_id=1, source_target_pairs={{0,1},{3,2},{4,5},{7,6},{8,9},{11,10},{12,13},{15,14},{16,17},{19,... | collective-permute-start | bytes 1179656 | tf_op jit(solution)/shard_map/ppermute | solution.py:422
  94.1 10.7 %collective-permute-start.20 = (bf16[64,2560]{1,0:T(8,128)(2,1)S(1)}, bf16[64,2560]{1,0:T(8,128)(2,1)S(1)}, u32[]{:S(2)}, u32[]{:S(2)}) collective-permute-start(bf16[64,2560]{1,0:T(8,128)(2,1)S(1)} %shard_map.211), channel_id=1, source_target_pairs={{1,2},{2,1},{5,6},{6,5},{9,10},{10,9},{13,14},{14,13},{17,18},{18,... | collective-permute-start | bytes 983048 | tf_op jit(solution)/shard_map/ppermute | solution.py:422
  94.8 10.8 %collective-permute-start.13 = (bf16[64,1536]{1,0:T(8,128)(2,1)S(1)}, bf16[64,1536]{1,0:T(8,128)(2,1)S(1)}, u32[]{:S(2)}, u32[]{:S(2)}) collective-permute-start(bf16[64,1536]{1,0:T(8,128)(2,1)S(1)} %get-tuple-element.54), channel_id=1, source_target_pairs={{0,8},{4,12},{8,0},{12,4},{16,24},{20,28},{24,16},{28,20},{1,9},{5... | collective-permute-start | bytes 589832 | tf_op jit(solution)/shard_map/ppermute | solution.py:474
  111.2 49.3 %all-to-all-start.1 = ((bf16[32,8,1152]{2,1,0:T(8,128)(2,1)}), bf16[32,8,1152]{2,1,0:T(8,128)(2,1)}, u32[]{:S(2)}, u32[]{:S(2)}) async-start(bf16[32,8,1152]{2,1,0:T(8,128)(2,1)} %bitcast.10), calls=%async_computation.1 | async-start | bytes 1179648 | tf_op jit(solution)/shard_map/all_to_all | solution.py:581
  115.0 17.1 %collective-permute-start.22 = (bf16[64,2560]{1,0:T(8,128)(2,1)S(1)}, bf16[64,2560]{1,0:T(8,128)(2,1)S(1)}, u32[]{:S(2)}, u32[]{:S(2)}) collective-permute-start(bf16[64,2560]{1,0:T(8,128)(2,1)S(1)} %copy-done.10), channel_id=1, source_target_pairs={{0,1},{3,2},{4,5},{7,6},{8,9},{11,10},{12,13},{15,14},{16,17},{19,... | collective-permute-start | bytes 983048 | tf_op jit(solution)/shard_map/ppermute | solution.py:422
  119.4 14.2 %collective-permute-start.26 = (bf16[64,3072]{1,0:T(8,128)(2,1)S(1)}, bf16[64,3072]{1,0:T(8,128)(2,1)S(1)}, u32[]{:S(2)}, u32[]{:S(2)}) collective-permute-start(bf16[64,3072]{1,0:T(8,128)(2,1)S(1)} %shard_map.218), channel_id=1, source_target_pairs={{1,2},{2,1},{5,6},{6,5},{9,10},{10,9},{13,14},{14,13},{17,18},{18,... | collective-permute-start | bytes 1179656 | tf_op jit(solution)/shard_map/ppermute | solution.py:422
  120.1 15.4 %collective-permute-start.24 = (bf16[64,2560]{1,0:T(8,128)(2,1)S(1)}, bf16[64,2560]{1,0:T(8,128)(2,1)S(1)}, u32[]{:S(2)}, u32[]{:S(2)}) collective-permute-start(bf16[64,2560]{1,0:T(8,128)(2,1)S(1)} %copy-done.24), channel_id=1, source_target_pairs={{1,0},{2,3},{5,4},{6,7},{9,8},{10,11},{13,12},{14,15},{17,16},{18,... | collective-permute-start | bytes 983048 | tf_op jit(solution)/shard_map/ppermute | solution.py:422
  134.1 17.5 %collective-permute-start.27 = (bf16[64,3072]{1,0:T(8,128)(2,1)S(1)}, bf16[64,3072]{1,0:T(8,128)(2,1)S(1)}, u32[]{:S(2)}, u32[]{:S(2)}) collective-permute-start(bf16[64,3072]{1,0:T(8,128)(2,1)S(1)} %shard_map.219), channel_id=1, source_target_pairs={{1,0},{2,3},{5,4},{6,7},{9,8},{10,11},{13,12},{14,15},{17,16},{18,... | collective-permute-start | bytes 1179656 | tf_op jit(solution)/shard_map/ppermute | solution.py:422
  139.8 18.3 %collective-permute-start.25 = (bf16[64,2560]{1,0:T(8,128)(2,1)S(1)}, bf16[64,2560]{1,0:T(8,128)(2,1)S(1)}, u32[]{:S(2)}, u32[]{:S(2)}) collective-permute-start(bf16[64,2560]{1,0:T(8,128)(2,1)S(1)} %shard_map.217), channel_id=1, source_target_pairs={{1,0},{2,3},{5,4},{6,7},{9,8},{10,11},{13,12},{14,15},{17,16},{18,... | collective-permute-start | bytes 983048 | tf_op jit(solution)/shard_map/ppermute | solution.py:422
  (43 other events, 236.1 us)
